TPU v7x, 32 devices: a whole 2x2x4 slice. The times are simulated.
32 devices in a mesh: ha: 16 (over z, x, core), wa: 2 (over y).
Axes of the slice: x: 2, y: 2, z: 4, core: 2. Of those that a mesh axis runs over, the one named last changes fastest.
Arguments:
- queries: bfloat16 [256, 128, 384], P('ha', 'wa'), may hold values from -200 to 200
- key_tokens: bfloat16 [256, 128, 384], P('ha', 'wa'), may hold values from -6 to 6
- value_tokens: bfloat16 [256, 128, 384], P('ha', 'wa'), may hold values from -6 to 6
- out_grad: bfloat16 [256, 128, 384], P('ha', 'wa'), may hold values from -96 to 96
- key_kernel: bfloat16 [3, 3, 384], replicated, may hold values from -2 to 2
- value_kernel: bfloat16 [3, 3, 384], replicated, may hold values from -2 to 2
- height_table: bfloat16 [511, 96], replicated, may hold values from -0.8984375 to 0.8984375
- width_table: bfloat16 [255, 96], replicated, may hold values from -0.8984375 to 0.8984375
Outputs:
- query_grad: bfloat16 [256, 128, 384], P('ha', 'wa')
- key_grad: bfloat16 [256, 128, 384], P('ha', 'wa')
- value_grad: bfloat16 [256, 128, 384], P('ha', 'wa')
- height_grad: float32 [511, 96], replicated
- width_grad: float32 [255, 96], replicated
All inputs are finite; a program needn't handle non-finite values.
Results may differ from a plain program's by a relative error of at most 0.02.
The roundings to bfloat16 on the way count: a program that leaves them out, or rounds other values in their place, can miss the bound.
Values may be sent and summed in bfloat16 or wider, within the bound.
A program may use at most 128 MiB of HBM per device.

v0:
```python
import jax
import jax.numpy as jnp
from jax import lax
from jax.sharding import PartitionSpec as P

HEADS = 4
HD = 96
KS = 3
STRIDE = 16


highest = lax.Precision.HIGHEST


def from_behind(block, axis, distance):
    devices = range(lax.axis_size(axis))
    route = [(i - distance, i) for i in devices if i - distance in devices]
    return lax.ppermute(block, axis, route)


def pool_partial(tokens, kernel):
    halfwidth = KS // 2
    pooled = lax.conv_general_dilated(
        tokens[None],
        kernel.astype(jnp.float32)[:, :, None, :],
        (STRIDE, STRIDE),
        ((halfwidth, halfwidth + 1), (halfwidth, halfwidth + 1)),
        dimension_numbers=("NHWC", "HWIO", "NHWC"),
        feature_group_count=tokens.shape[-1],
        precision=highest,
    )
    return pooled[0]


def on_device(
    queries, key_tokens, value_tokens, out_grad, key_kernel, value_kernel, height_table, width_table
):
    own_rows, own_cols, width_all = queries.shape
    pooled_rows = own_rows // STRIDE
    pooled_cols = own_cols // STRIDE
    rows_axis = lax.axis_size("ha")
    cols_axis = lax.axis_size("wa")
    key_rows = pooled_rows * rows_axis
    key_cols = pooled_cols * cols_axis
    key_count = key_rows * key_cols
    score_scale = HD ** (-0.5)
    key_float = key_tokens.astype(jnp.float32)
    value_float = value_tokens.astype(jnp.float32)
    partial_value = jnp.stack(
        [pool_partial(key_float, key_kernel), pool_partial(value_float, value_kernel)]
    )
    from_above = from_behind(partial_value[:, pooled_rows:], "ha", 1)
    own_part = jnp.concatenate(
        [partial_value[:, 0:1] + from_above, partial_value[:, 1:pooled_rows]], 1
    )
    from_left = from_behind(own_part[:, :, pooled_cols:], "wa", 1)
    pooled = jnp.concatenate(
        [own_part[:, :, 0:1] + from_left, own_part[:, :, 1:pooled_cols]], 2
    ).astype(jnp.bfloat16)
    flattened = pooled.reshape(2, pooled_rows * pooled_cols, width_all)
    gathered = lax.all_gather(flattened, ("ha", "wa"), axis=1, tiled=True)
    gathered = gathered.reshape(
        2, rows_axis, cols_axis, pooled_rows, pooled_cols, width_all
    ).transpose(0, 1, 3, 2, 4, 5)
    all_keys = gathered.reshape(2, key_count, HEADS, HD)
    key_heads = all_keys[0]
    value_heads = all_keys[1]
    row_first = lax.axis_index("ha") * own_rows
    col_first = lax.axis_index("wa") * own_cols
    height_index = (
        row_first
        + jnp.arange(own_rows, dtype=jnp.int32)[:, None]
        - STRIDE * jnp.arange(key_rows, dtype=jnp.int32)[None, :]
        + (key_rows - 1) * STRIDE
    )
    width_index = (
        col_first
        + jnp.arange(own_cols, dtype=jnp.int32)[:, None]
        - STRIDE * jnp.arange(key_cols, dtype=jnp.int32)[None, :]
        + (key_cols - 1) * STRIDE
    )
    height_onehot = (
        height_index.reshape(-1, 1) == jnp.arange(height_table.shape[0], dtype=jnp.int32)[None, :]
    ).astype(jnp.bfloat16)
    width_onehot = (
        width_index.reshape(-1, 1) == jnp.arange(width_table.shape[0], dtype=jnp.int32)[None, :]
    ).astype(jnp.bfloat16)
    height_rows = (
        jnp.dot(height_onehot, height_table, preferred_element_type=jnp.float32)
        .astype(jnp.bfloat16)
        .reshape(own_rows, key_rows, HD)
    )
    width_rows = (
        jnp.dot(width_onehot, width_table, preferred_element_type=jnp.float32)
        .astype(jnp.bfloat16)
        .reshape(own_cols, key_cols, HD)
    )
    query_heads = queries.reshape(own_rows, own_cols, HEADS, HD)
    rel_height = jnp.einsum(
        "rwnd,rkd->rwnk", query_heads, height_rows, preferred_element_type=jnp.float32
    )
    rel_width = jnp.einsum(
        "rwnd,wkd->rwnk", query_heads, width_rows, preferred_element_type=jnp.float32
    )
    token_count = own_rows * own_cols
    block_size = min(512, token_count)
    block_count = token_count // block_size
    query_flat = queries.reshape(token_count, HEADS, HD)
    grad_flat = out_grad.reshape(token_count, HEADS, HD)
    height_flat = rel_height.reshape(token_count, HEADS, key_rows)
    width_flat = rel_width.reshape(token_count, HEADS, key_cols)

    def block_step(totals, block_index):
        key_acc, value_acc = totals
        first_token = block_index * block_size
        query_block = lax.dynamic_slice_in_dim(query_flat, first_token, block_size, 0)
        grad_block = lax.dynamic_slice_in_dim(grad_flat, first_token, block_size, 0)
        height_block = lax.dynamic_slice_in_dim(height_flat, first_token, block_size, 0)
        width_block = lax.dynamic_slice_in_dim(width_flat, first_token, block_size, 0)
        score_bias = (height_block[..., :, None] + width_block[..., None, :]).reshape(
            block_size, HEADS, key_count
        )
        scores = (
            score_scale
            * jnp.einsum("tnd,knd->tnk", query_block, key_heads, preferred_element_type=jnp.float32)
            + score_bias
        )
        scores = scores - jnp.max(scores, axis=-1, keepdims=True)
        weights = jnp.exp(scores)
        attention = weights / jnp.sum(weights, axis=-1, keepdims=True)
        probs_low = attention.astype(jnp.bfloat16)
        attended = jnp.einsum(
            "tnk,knd->tnd", probs_low, value_heads, preferred_element_type=jnp.float32
        )
        grad_probs = jnp.einsum(
            "tnd,knd->tnk", grad_block, value_heads, preferred_element_type=jnp.float32
        )
        row_delta = jnp.sum(grad_block.astype(jnp.float32) * attended, axis=-1, keepdims=True)
        grad_scores = attention * (grad_probs - row_delta)
        grad_low = grad_scores.astype(jnp.bfloat16)
        query_attn = score_scale * jnp.einsum(
            "tnk,knd->tnd", grad_low, key_heads, preferred_element_type=jnp.float32
        )
        key_acc = key_acc + score_scale * jnp.einsum(
            "tnk,tnd->knd", grad_low, query_block, preferred_element_type=jnp.float32
        )
        value_acc = value_acc + jnp.einsum(
            "tnk,tnd->knd", probs_low, grad_block, preferred_element_type=jnp.float32
        )
        score_grid = grad_scores.reshape(block_size, HEADS, key_rows, key_cols)
        return (
            (key_acc, value_acc),
            (query_attn, jnp.sum(score_grid, axis=-1), jnp.sum(score_grid, axis=-2)),
        )

    initial = (
        jnp.zeros((key_count, HEADS, HD), jnp.float32),
        jnp.zeros((key_count, HEADS, HD), jnp.float32),
    )
    totals, results = lax.scan(block_step, initial, jnp.arange(block_count, dtype=jnp.int32))
    query_attn = results[0].reshape(own_rows, own_cols, HEADS, HD)
    grad_height = results[1].reshape(own_rows, own_cols, HEADS, key_rows)
    grad_width = results[2].reshape(own_rows, own_cols, HEADS, key_cols)
    query_rel = jnp.einsum(
        "rwnk,rkd->rwnd", grad_height, height_rows.astype(jnp.float32), precision=highest
    ) + jnp.einsum("rwnk,wkd->rwnd", grad_width, width_rows.astype(jnp.float32), precision=highest)
    query_grad = (
        (query_attn + query_rel).reshape(own_rows, own_cols, width_all).astype(jnp.bfloat16)
    )
    query_float = query_heads.astype(jnp.float32)
    height_local = jnp.einsum(
        "rwnk,rwnd->rkd", grad_height, query_float, precision=highest
    ).reshape(own_rows * key_rows, HD)
    width_local = jnp.einsum("rwnk,rwnd->wkd", grad_width, query_float, precision=highest).reshape(
        own_cols * key_cols, HD
    )
    height_grad = jnp.dot(height_onehot.astype(jnp.float32).T, height_local, precision=highest)
    width_grad = jnp.dot(width_onehot.astype(jnp.float32).T, width_local, precision=highest)
    height_grad, width_grad = lax.psum((height_grad, width_grad), ("ha", "wa"))
    key_sums = jnp.stack([totals[0], totals[1]]).reshape(2, key_rows, key_cols, width_all)
    arranged = key_sums.reshape(
        2, rows_axis, pooled_rows, cols_axis, pooled_cols, width_all
    ).transpose(0, 1, 3, 2, 4, 5)
    arranged = arranged.reshape(2, rows_axis * cols_axis * pooled_rows * pooled_cols, width_all)
    own_sums = lax.psum_scatter(arranged, ("ha", "wa"), scatter_dimension=1, tiled=True).reshape(
        2, pooled_rows, pooled_cols, width_all
    )
    from_right = from_behind(own_sums[:, :, 0:1], "wa", -1)
    widened = jnp.concatenate([own_sums, from_right], 2)
    from_below = from_behind(widened, "ha", -1)
    cotangent = jnp.concatenate([widened, from_below], 1)
    _, key_back = jax.vjp(lambda tokens: pool_partial(tokens, key_kernel), key_float)
    key_grad = key_back(cotangent[0])[0].astype(jnp.bfloat16)
    _, value_back = jax.vjp(lambda tokens: pool_partial(tokens, value_kernel), value_float)
    value_grad = value_back(cotangent[1])[0].astype(jnp.bfloat16)
    return (query_grad, key_grad, value_grad, height_grad, width_grad)


def solution(mesh):
    placed = (
        P("ha", "wa", None),
        P("ha", "wa", None),
        P("ha", "wa", None),
        P("ha", "wa", None),
        P(),
        P(),
        P(),
        P(),
    )
    return jax.shard_map(
        on_device,
        mesh=mesh,
        in_specs=placed,
        out_specs=(P("ha", "wa", None), P("ha", "wa", None), P("ha", "wa", None), P(), P()),
        check_vma=False,
    )
```

profile of v0, /device:TPU:0, one launch (start us, length us, event | category | flops | bytes accessed | tf_op | source)
XLA Modules:
  0.0 296.9 jit_solution(10031842348520160365)
XLA Ops:
  7.2 1.5 pad
  8.7 0.4 copy.86
  9.2 0.7 copy-done.2
  9.9 0.4 pad.2
  10.3 0.4 copy.91
  10.9 1.0 fusion.56
  12.0 1.1 fusion.65
  13.1 2.4 collective-permute-start
  16.8 0.6 reshape.151
  17.4 2.6 convolution_bitcast_fusion.3
  20.0 0.9 convolution_bitcast_fusion.4
  20.9 3.3 %reshape.149 = bf16[1024,4,96]{2,1,0:T(4,128)(2,1)} reshape(bf16[16,64,384]{2,1,0:T(8,128)(2,1)} %param.10) | data formatting | bytes 1572864 | tf_op jit(solution)/shard_map/reshape | solution.py:108
  24.2 1.1 copy.99
  25.3 1.2 reshape.152
  26.5 0.6 copy.102
  27.2 2.5 reshape.155
  29.7 1.4 copy.105
  31.1 1.6 copy.104
  32.7 4.3 %collective-permute-start.1 = (f32[2,1,1,384]{3,2,1,0:T(1,128)S(1)}, f32[2,1,1,384]{3,2,1,0:T(1,128)S(1)}, u32[]{:S(2)}, u32[]{:S(2)}) collective-permute-start(f32[2,1,1,384]{3,2,1,0:T(1,128)S(1)} %slice.54), channel_id=1, source_target_pairs={{0,1},{2,3},{4,5},{6,7},{8,9},{10,11},{12,13},{14,15},{16,17},{18,... | collective-permute-start | bytes 9224 | tf_op jit(solution)/shard_map/ppermute | solution.py:18
  37.0 1.3 collective-permute-done.1
  38.3 68.6 %all_gather.3 = bf16[2,128,384]{2,0,1:T(2,128)(2,1)S(1)} all-gather(bf16[2,4,384]{2,0,1:T(2,128)(2,1)S(1)} %copy.95), channel_id=1, replica_groups=mesh['ha'=16,'wa'=2] {'ha','wa'}, dimensions={1}, use_global_device_ids=true | all-gather | bytes 202752 | tf_op jit(solution)/shard_map/all_gather | solution.py:61
  107.2 0.8 copy.136
  108.1 27.7 %while.19 = (s32[]{:T(128)}, f32[128,4,96]{0,2,1:T(8,128)S(1)}, f32[128,4,96]{0,2,1:T(8,128)}, f32[2,512,4,96]{1,3,2,0:T(8,128)}, f32[2,512,4,16]{1,0,3,2:T(2,12...) while((s32[]{:T(128)}, f32[128,4,96]{0,2,1:T(8,128)S(1)}, ...), condition=%wide.region_6.7_spmd.clone, body=%wide.region_0.6_spmd.clone.sunk | while | flops 306903168 | bytes 19055068 | solution.py:160
  108.2 0.6 dynamic_slice.55
  109.4 1.5 fusion.148
  110.9 1.7 fusion.149
  112.8 1.0 fusion.151
  113.8 0.6 bitcast_reduce_fusion.3
  114.7 2.0 dynamic_update_slice.21
  116.6 3.4 %dynamic_update_slice.20 = f32[2,512,4,16]{1,0,3,2:T(2,128)} dynamic-update-slice(f32[2,512,4,16]{1,0,3,2:T(2,128)} %get-tuple-element.315, f32[1,512,4,16]{1,0,3,2:T(1,128)S(1)} %copy.165, s32[]{:T(128)S(6)} %copy.176, s32[]{:T(128)} %constant.24.clone.1..sunk, s32[]{:T(128)} %constant.24.clone.1..sunk, s32[]{:T(128)} %constant.24.clone.1..sunk) | dynamic-update-slice | bytes 262148 | tf_op jit(solution)/shard_map/while/body/jit(dynamic_update_index_in_dim)/dynamic_update_slice | solution.py:160
  120.0 0.3 fusion.150
  120.4 1.2 fusion.152
  121.6 0.6 dynamic_slice.55
  122.8 1.5 fusion.148
  124.3 1.7 fusion.149
  126.2 1.9 fusion.151
  128.1 0.6 bitcast_reduce_fusion.3
  128.9 2.0 dynamic_update_slice.21
  130.9 3.4 %dynamic_update_slice.20 = f32[2,512,4,16]{1,0,3,2:T(2,128)} dynamic-update-slice(f32[2,512,4,16]{1,0,3,2:T(2,128)} %get-tuple-element.315, f32[1,512,4,16]{1,0,3,2:T(1,128)S(1)} %copy.165, s32[]{:T(128)S(6)} %copy.176, s32[]{:T(128)} %constant.24.clone.1..sunk, s32[]{:T(128)} %constant.24.clone.1..sunk, s32[]{:T(128)} %constant.24.clone.1..sunk) | dynamic-update-slice | bytes 262148 | tf_op jit(solution)/shard_map/while/body/jit(dynamic_update_index_in_dim)/dynamic_update_slice | solution.py:160
  134.3 0.3 fusion.150
  134.7 1.1 fusion.152
  135.8 1.0 pad_maximum_fusion
  136.8 0.9 copy.114
  137.8 1.1 reshape.158
  139.2 0.7 fusion.70
  139.8 1.1 fusion.76
  140.9 0.9 copy.110
  141.8 2.2 convolution_bitcast_fusion.5
  144.1 1.1 fusion.75
  145.5 123.8 %all-reduce.4.cloned.1.call-done = (f32[2,128,384]{2,0,1:T(2,128)}, f32[511,96]{0,1:T(8,128)}, f32[255,96]{0,1:T(8,128)}) async-done(((f32[2,128,384]{2,0,1:T(2,128)}, f32[511,96]{0,1:T(8,128)}, f32[255,96]{0,1:T(8,128)}), (f32[2,128,384]{2,0,1:T(2,128)}, f32[511,96]{0,1:T(8,128)}, f32[255,96]{0,1:T(8,128)})) %all-reduce.4.cloned.1.call-update) | async-done | bytes 687376
  269.3 0.7 dynamic-slice_bitcast_fusion
  270.0 1.3 collective-permute-start.2
  271.3 3.3 %fusion.83 = f32[64,96,16,4]{1,2,3,0:T(8,128)} fusion(f32[16,64,4,8]{0,3,2,1:T(8,128)S(1)} %copy.110, bf16[512,96]{1,0:T(8,128)(2,1)S(1)} %copy.100), kind=kOutput, calls=%fused_computation.89 | convolution fusion | flops 37748736 | bytes 1802240 | tf_op jit(solution)/shard_map/rwnk,wkd->rwnd/dot_general | solution.py:166
  274.5 1.8 copy.106
  276.4 1.5 collective-permute-start.3
  277.9 4.4 %fusion.38 = bf16[16,64,4,96]{3,1,2,0:T(8,128)(2,1)S(1)} fusion(f32[16,64,4,96]{3,1,0,2:T(8,128)S(1)} %bitcast.200, f32[64,96,16,4]{1,2,3,0:T(8,128)} %fusion.83, bf16[16,16,96,1]{2,1,3,0:T(8,128)(2,1)S(1)} %bitcast.212, f32[16,64,4,16]{1,0,3,2:T(8,128)S(1)} %reshape.157), kind=kOutput, calls=%fused_computation.44 | convolution fusion | flops 76677120 | bytes 4243456 | tf_op jit(solution)/shard_map/rwnk,rkd->rwnd/dot_general | solution.py:164
  282.3 0.9 copy.113
  283.2 1.6 convert_element_type.57
  284.8 0.9 convolution_convert_fusion
  285.7 1.1 copy.161
  286.7 0.9 convolution_convert_fusion.1
  287.6 1.1 copy.162
  288.7 0.7 copy.191
  289.4 0.6 copy.192
  (94 shorter events, 3.7 us)
Async XLA Ops:
  7.2 8.7 %copy-start = (bf16[511,96]{0,1:T(8,128)(2,1)S(1)}, bf16[511,96]{0,1:T(8,128)(2,1)}, u32[]{:S(2)}) copy-start(bf16[511,96]{0,1:T(8,128)(2,1)} %param.16) | copy-start | bytes 294340
  7.2 262.1 %all-reduce.4.cloned.1.call-start = ((), (), s32[]{:S(2)}) async-start(), calls=%async_computation | async-start | bytes 1376256
  8.7 1.1 copy-start.2
  10.2 0.7 copy-start.8
  10.3 0.7 copy-start.13
  10.7 1.3 copy-start.9
  10.9 5.4 %copy-start.14 = (bf16[255,96]{0,1:T(8,128)(2,1)S(1)}, bf16[255,96]{0,1:T(8,128)(2,1)}, u32[]{:S(2)}) copy-start(bf16[255,96]{0,1:T(8,128)(2,1)} %param.17) | copy-start | bytes 146884
  11.9 4.9 %copy-start.1 = (bf16[16,64,384]{2,1,0:T(8,128)(2,1)S(1)}, bf16[16,64,384]{2,1,0:T(8,128)(2,1)}, u32[]{:S(2)}) copy-start(bf16[16,64,384]{2,1,0:T(8,128)(2,1)} %param.10) | copy-start | bytes 2359300
  13.1 19.5 %collective-permute-start = (f32[2,1,5,384]{3,2,1,0:T(8,128)S(1)}, f32[2,1,5,384]{3,2,1,0:T(8,128)S(1)}, u32[]{:S(2)}, u32[]{:S(2)}) collective-permute-start(f32[2,1,5,384]{3,2,1,0:T(8,128)S(1)} %pad_maximum_fusion.2), channel_id=1, source_target_pairs={{0,2},{2,4},{4,6},{6,8},{8,10},{10,12},{12,14},{14,16},{16,18},{18... | collective-permute-start | bytes 46088 | tf_op jit(solution)/shard_map/ppermute | solution.py:18
  15.7 0.5 copy-start.11
  32.7 5.6 %collective-permute-start.1 = (f32[2,1,1,384]{3,2,1,0:T(1,128)S(1)}, f32[2,1,1,384]{3,2,1,0:T(1,128)S(1)}, u32[]{:S(2)}, u32[]{:S(2)}) collective-permute-start(f32[2,1,1,384]{3,2,1,0:T(1,128)S(1)} %slice.54), channel_id=1, source_target_pairs={{0,1},{2,3},{4,5},{6,7},{8,9},{10,11},{12,13},{14,15},{16,17},{18,... | collective-permute-start | bytes 9224 | tf_op jit(solution)/shard_map/ppermute | solution.py:18
  108.2 5.7 %copy-start.15 = (s32[2]{0:T(128)}, s32[2]{0:T(128)S(1)}, u32[]{:S(2)}) copy-start(s32[2]{0:T(128)S(1)} %get-tuple-element.334) | copy-start | bytes 28 | tf_op jit(solution)/shard_map/while
  108.2 2.8 copy-start.7
  110.9 1.7 copy-start.3
  110.9 1.9 copy-start.17
  120.0 1.5 copy-start.16
  121.5 6.6 %copy-start.15 = (s32[2]{0:T(128)}, s32[2]{0:T(128)S(1)}, u32[]{:S(2)}) copy-start(s32[2]{0:T(128)S(1)} %get-tuple-element.334) | copy-start | bytes 28 | tf_op jit(solution)/shard_map/while
  121.5 2.7 copy-start.7
  124.3 1.7 copy-start.3
  124.3 1.9 copy-start.17
  134.3 1.5 copy-start.16
  135.8 3.0 %copy-start.4 = (f32[2,512,4,16]{1,0,3,2:T(2,128)S(1)}, f32[2,512,4,16]{1,0,3,2:T(2,128)}, u32[]{:S(2)}) copy-start(f32[2,512,4,16]{1,0,3,2:T(2,128)} %get-tuple-element.77) | copy-start | bytes 786436
  136.8 3.0 %copy-start.12 = (s32[256]{0:T(256)S(1)}, s32[256]{0:T(256)}, u32[]{:S(2)}) copy-start(s32[256]{0:T(256)} %copy-done.11) | copy-start | bytes 3076
  141.8 3.5 %copy-start.10 = (bf16[3,3,384]{2,1,0:T(4,128)(2,1)S(1)}, bf16[3,3,384]{2,1,0:T(4,128)(2,1)}, u32[]{:S(2)}) copy-start(bf16[3,3,384]{2,1,0:T(4,128)(2,1)} %param.15) | copy-start | bytes 20740
  270.0 6.4 %collective-permute-start.2 = (f32[2,1,1,384]{3,0,2,1:T(2,128)S(1)}, f32[2,1,1,384]{3,0,2,1:T(2,128)S(1)}, u32[]{:S(2)}, u32[]{:S(2)}) collective-permute-start(f32[2,1,1,384]{3,0,2,1:T(2,128)S(1)} %slice.58), channel_id=1, source_target_pairs={{1,0},{3,2},{5,4},{7,6},{9,8},{11,10},{13,12},{15,14},{17,16},{19,... | collective-permute-start | bytes 9224 | tf_op jit(solution)/shard_map/ppermute | solution.py:18
  276.4 8.4 %collective-permute-start.3 = (f32[2,1,5,384]{3,0,2,1:T(2,128)S(1)}, f32[2,1,5,384]{3,0,2,1:T(2,128)S(1)}, u32[]{:S(2)}, u32[]{:S(2)}) collective-permute-start(f32[2,1,5,384]{3,0,2,1:T(2,128)S(1)} %pad_maximum_fusion.3), channel_id=1, source_target_pairs={{2,0},{4,2},{6,4},{8,6},{10,8},{12,10},{14,12},{16,14},{18,16},{20... | collective-permute-start | bytes 46088 | tf_op jit(solution)/shard_map/ppermute | solution.py:18
  287.6 1.1 copy-start.5
  287.6 1.7 copy-start.6
Sparse Core Ops, SparseCore 0:
  145.3 123.8 all-reduce.3
where the time goes:
time: 301 us; the launch traced here: 297 us
  waiting for transfers between devices  125 us (42%)
  blocking collectives  68.6 us (23%)
  local copies, waits for them, and re-layouts  42.4 us (14%)
  matrix products  34.2 us (11%)
  between operations  14.5 us (5%)
  starting transfers between devices  9.44 us (3%)
    unnamed x2, waiting for transfers between devices  124 us
    all_gather x1, blocking collectives, on_device(): gathered = lax.all_gather(flattened, ('ha', 'wa'), axis=1, tiled=True)  68.6 us
    dynamic_update_slice x8, local copies, waits for them, and re-layouts, on_device(): lax.scan(block_step, initial, jnp.arange(block_count, dtype=jnp.int32))  11.2 us
    ppermute x4, starting transfers between devices, from_behind(): return lax.ppermute(block, axis, route)  9.41 us
    unnamed x34, local copies, waits for them, and re-layouts  8.37 us
  transfers between devices with their start and end apart: 5, of which 2 were waited for; matrix products, arithmetic and copies ran while one was open for 10% of the time, Pallas kernels for 0%

commit v1 on v0

v1 whole, which is shorter than its diff:
```python
import functools

import jax
import jax.numpy as jnp
from jax import lax
from jax.experimental import pallas as pl
from jax.experimental.pallas import tpu as pltpu
from jax.sharding import PartitionSpec as P

HEADS = 4
HD = 96
KS = 3
STRIDE = 16
MESH = pl.DeviceIdType.MESH
F32 = jnp.float32
BF16 = jnp.bfloat16


def round_up(value, unit):
    return -(-value // unit) * unit


def greet(to_each, count):
    barrier = pltpu.get_barrier_semaphore()
    to_each(lambda device: pl.semaphore_signal(barrier, 1, device_id=device, device_id_type=MESH))
    pl.semaphore_wait(barrier, count)


def gather_kernel(
    n_ha, n_wa, pc,
    key_hbm, value_hbm, key_kernel, value_kernel, gathered,
    tokens, part, arrived, load_sem, own_send, own_recv, next_send, next_recv, row_send, row_recv,
):
    r = lax.axis_index("ha")
    w = lax.axis_index("wa")
    span = part.shape[2]
    kc = pc * n_wa
    last = tokens.shape[2] // pc
    has_next = r + 1 < n_ha
    has_prev = r > 0

    loads = []
    for a, source in enumerate((key_hbm, value_hbm)):
        loads.append(
            pltpu.make_async_copy(
                source.at[pl.ds(0, 2)], tokens.at[a, pl.ds(0, 2)], load_sem.at[2 * a]
            )
        )
        loads.append(
            pltpu.make_async_copy(
                source.at[pl.ds(STRIDE - 1, 1)], tokens.at[a, pl.ds(2, 1)], load_sem.at[2 * a + 1]
            )
        )
    for load in loads:
        load.start()

    barrier = pltpu.get_barrier_semaphore()

    @pl.loop(1, n_ha)
    def _(d):
        pl.semaphore_signal(
            barrier, 1, device_id=(lax.rem(r + d, n_ha), w), device_id_type=MESH
        )

    for d in range(1, n_wa):
        other = lax.rem(w + d, n_wa)
        pl.semaphore_signal(barrier, 1, device_id=(r, other), device_id_type=MESH)

        @pl.when(has_next)
        def _():
            pl.semaphore_signal(barrier, 1, device_id=(r + 1, other), device_id_type=MESH)

        @pl.when(has_prev)
        def _():
            pl.semaphore_signal(barrier, 1, device_id=(r - 1, other), device_id_type=MESH)

    extra = jnp.where(has_next, n_wa - 1, 0) + jnp.where(has_prev, n_wa - 1, 0)

    for load in loads:
        load.wait()

    def pooled(a, kernel, uses):
        rows = [None] * (pc + 1)

        def add(k, term):
            rows[k] = term if rows[k] is None else rows[k] + term

        for at, tap in uses:
            line = tokens[a, at].astype(F32)
            for k in range(pc):
                for col, to, key in ((0, 1, k), (1, 2, k), (STRIDE - 1, 0, k + 1)):
                    at_col = STRIDE * k + col
                    weight = kernel[tap, to : to + 1].astype(F32)
                    add(key, line[at_col : at_col + 1] * weight)
        return jnp.concatenate(
            rows + [jnp.zeros((span - pc - 1, tokens.shape[-1]), F32)], 0
        )

    for a, kernel in enumerate((key_kernel, value_kernel)):
        part[0, a] = pooled(a, kernel, ((0, 1), (1, 2)))
        part[1, a] = pooled(a, kernel, ((2, 0),))

    pl.semaphore_wait(barrier, n_ha - 1 + n_wa - 1 + extra)

    def own_copy(target, slot):
        return pltpu.make_async_remote_copy(
            src_ref=part.at[0],
            dst_ref=arrived.at[0, slot],
            send_sem=own_send.at[target],
            recv_sem=own_recv.at[slot],
            device_id=(r, target),
            device_id_type=MESH,
        )

    def next_copy(target, slot):
        return pltpu.make_async_remote_copy(
            src_ref=part.at[1],
            dst_ref=arrived.at[1, slot],
            send_sem=next_send.at[target],
            recv_sem=next_recv.at[slot],
            device_id=(r + 1, target),
            device_id_type=MESH,
        )

    for d in range(1, n_wa):
        own_copy(lax.rem(w + d, n_wa), w).start()

    @pl.when(has_next)
    def _():
        for d in range(n_wa):
            next_copy(lax.rem(w + d, n_wa), w).start()

    arrived[0, pl.ds(w, 1)] = part[0:1]

    @pl.when(r == 0)
    def _():
        arrived[1] = jnp.zeros_like(arrived[1])

    for d in range(1, n_wa):
        own_copy(lax.rem(w + d, n_wa), lax.rem(w + n_wa - d, n_wa)).wait_recv()

    @pl.when(has_prev)
    def _():
        for d in range(n_wa):
            next_copy(lax.rem(w + d, n_wa), lax.rem(w + n_wa - d, n_wa)).wait_recv()

    halves = []
    for a in range(2):
        blocks = []
        carried = None
        for c in range(n_wa):
            block = arrived[0, c, a] + arrived[1, c, a]
            if carried is not None:
                block = jnp.concatenate([block[0:1] + carried, block[1:]], 0)
            carried = block[pc : pc + 1]
            blocks.append(block[0:pc])
        halves.append(jnp.concatenate(blocks, 0))
    gathered[pl.ds(r, 1)] = jnp.concatenate(halves, 0).astype(BF16)[None]

    def row_copy(target, slot):
        return pltpu.make_async_remote_copy(
            src_ref=gathered.at[slot],
            dst_ref=gathered.at[slot],
            send_sem=row_send.at[target],
            recv_sem=row_recv.at[slot],
            device_id=(target, w),
            device_id_type=MESH,
        )

    @pl.loop(1, n_ha)
    def _(d):
        row_copy(lax.rem(r + d, n_ha), r).start()

    for d in range(1, n_wa):
        own_copy(lax.rem(w + d, n_wa), w).wait_send()

    @pl.when(has_next)
    def _():
        for d in range(n_wa):
            next_copy(lax.rem(w + d, n_wa), w).wait_send()

    @pl.loop(1, n_ha)
    def _(d):
        source = lax.rem(r + n_ha - d, n_ha)
        row_copy(source, source).wait_recv()

    @pl.loop(1, n_ha)
    def _(d):
        row_copy(lax.rem(r + d, n_ha), r).wait_send()


def gather_pooled(n_ha, n_wa, key_tokens, value_tokens, key_kernel, value_kernel):
    own_cols, width = key_tokens.shape[1:]
    pc = own_cols // STRIDE
    span = round_up(pc + 1, 8)
    dma = pltpu.SemaphoreType.DMA
    return pl.pallas_call(
        functools.partial(gather_kernel, n_ha, n_wa, pc),
        out_shape=jax.ShapeDtypeStruct((n_ha, 2 * pc * n_wa, width), BF16),
        in_specs=[pl.BlockSpec(memory_space=pl.ANY)] * 2
        + [pl.BlockSpec(memory_space=pltpu.VMEM)] * 2,
        out_specs=pl.BlockSpec(memory_space=pltpu.VMEM),
        scratch_shapes=[
            pltpu.VMEM((2, 3, own_cols, width), BF16),
            pltpu.VMEM((2, 2, span, width), F32),
            pltpu.VMEM((2, n_wa, 2, span, width), F32),
            dma((4,)),
            dma((n_wa,)),
            dma((n_wa,)),
            dma((n_wa,)),
            dma((n_wa,)),
            dma((n_ha,)),
            dma((n_ha,)),
        ],
        compiler_params=pltpu.CompilerParams(
            collective_id=0, has_side_effects=True, vmem_limit_bytes=32 * 2**20
        ),
        name="pool_gather",
    )(key_tokens, value_tokens, key_kernel, value_kernel)


def window(head):
    low = head * HD // 128 * 128
    high = round_up((head + 1) * HD, 128)
    return low, high


def nt(left, right):
    return lax.dot_general(left, right, (((1,), (1,)), ((), ())), preferred_element_type=F32)


def nn(left, right):
    return lax.dot_general(left, right, (((1,), (0,)), ((), ())), preferred_element_type=F32)


def tn(left, right):
    return lax.dot_general(left, right, (((0,), (0,)), ((), ())), preferred_element_type=F32)


def attention_kernel(
    n_ha, n_wa, pc, own_cols, tile_rows, rows_h,
    queries, out_grad, gathered, height_rows, width_rows,
    query_grad, sums, tables,
    key_win, value_win, height_win, width_win, main_acc, height_acc, value_acc,
    key_full, value_full, height_full, width_full, fold,
):
    kc = pc * n_wa
    kr = n_ha
    keys = kr * kc
    blocks = pc + kc - 1
    scale = HD ** (-0.5)
    tile = tile_rows * own_cols
    tiles = queries.shape[0] // tile
    hrows = tile_rows * kr

    lane = lax.broadcasted_iota(jnp.int32, (1, tile), 1)
    lane_row = lane // own_cols
    lane_col = lane % own_cols
    lane_block = lane_col // STRIDE
    lane_in = lane_col % STRIDE
    in_block = lax.broadcasted_iota(jnp.int32, (1, STRIDE, tile), 1) == lane_in[None]

    for head in range(HEADS):
        low, high = window(head)
        size = high - low
        channel = lax.broadcasted_iota(jnp.int32, (1, size), 1) + low
        mine = (channel >= head * HD) & (channel < (head + 1) * HD)
        zero = jnp.zeros((), BF16)

        pooled = gathered[:, :, low:high].astype(F32)
        pooled = jnp.where(mine[None], pooled, 0.0)
        key_win[:, :size] = pooled[:, :kc].reshape(keys, size).astype(BF16)
        value_win[:, :size] = pooled[:, kc:].reshape(keys, size).astype(BF16)
        height_win[:, :size] = jnp.where(mine, height_rows[:, low:high].astype(F32), 0.0).astype(
            BF16
        )
        width_win[:, :size] = jnp.where(mine, width_rows[:, low:high].astype(F32), 0.0).astype(BF16)

        def step(i, first):
            base = pl.multiple_of(i * tile, tile)
            hbase = pl.multiple_of(i * hrows, hrows)
            q = queries[pl.ds(base, tile), low:high]
            g = out_grad[pl.ds(base, tile), low:high]
            kw_ = key_win[:, :size]
            vw_ = value_win[:, :size]
            hw_ = height_win[pl.ds(hbase, hrows), :size]
            ww_ = width_win[:, :size]
            raw_h = nt(hw_, q)
            raw_w = nt(ww_, q)
            rel_h = raw_h[0:kr]
            for a in range(1, tile_rows):
                rel_h = jnp.where(lane_row == a, raw_h[a * kr : (a + 1) * kr], rel_h)
            picked = jnp.sum(
                jnp.where(in_block, raw_w.reshape(blocks, STRIDE, tile), 0.0), axis=1
            )
            rel_w = picked[pc - 1 : pc - 1 + kc]
            for u in range(1, pc):
                rel_w = jnp.where(lane_block == u, picked[pc - 1 - u : pc - 1 - u + kc], rel_w)
            scores = nt(kw_, q).reshape(kr, kc, tile) * scale + (rel_h[:, None, :] + rel_w[None])
            top = jnp.max(jnp.max(scores, axis=0), axis=0, keepdims=True)
            weights = jnp.exp(scores - top[None])
            total = jnp.sum(jnp.sum(weights, axis=0), axis=0, keepdims=True)
            probs = weights * (1.0 / total)[None]
            probs_low = probs.astype(BF16)
            grad_probs = nt(vw_, g).reshape(kr, kc, tile)
            delta = jnp.sum(
                jnp.sum(probs_low.astype(F32) * grad_probs, axis=0), axis=0, keepdims=True
            )
            grad_scores = probs * (grad_probs - delta[None])
            grad_low = grad_scores.astype(BF16).reshape(keys, tile)
            probs_low = probs_low.reshape(keys, tile)
            grad_h = jnp.sum(grad_scores, axis=1)
            grad_w = jnp.sum(grad_scores, axis=0)
            spread_h = jnp.concatenate(
                [jnp.where(lane_row == a, grad_h, 0.0) for a in range(tile_rows)], 0
            ).astype(BF16)
            shifted = None
            for u in range(pc):
                pieces = []
                if pc - 1 - u:
                    pieces.append(jnp.zeros((pc - 1 - u, tile), F32))
                pieces.append(jnp.where(lane_block == u, grad_w, 0.0))
                if u:
                    pieces.append(jnp.zeros((u, tile), F32))
                piece = jnp.concatenate(pieces, 0)
                shifted = piece if shifted is None else shifted + piece
            spread_w = (
                jnp.where(in_block, shifted[:, None, :], 0.0)
                .reshape(blocks * STRIDE, tile)
                .astype(BF16)
            )
            d_query = tn(grad_low, kw_) * scale + tn(
                jnp.concatenate([spread_h, spread_w], 0), jnp.concatenate([hw_, ww_], 0)
            )
            old = query_grad[pl.ds(base, tile), low:high]
            query_grad[pl.ds(base, tile), low:high] = jnp.where(
                mine, d_query, old.astype(F32)
            ).astype(BF16)
            by_query = nn(jnp.concatenate([grad_low, spread_w, spread_h], 0), q)
            by_grad = nn(probs_low, g)
            split = keys + blocks * STRIDE
            if first:
                main_acc[:, :size] = by_query[:split]
                value_acc[:, :size] = by_grad
            else:
                main_acc[:, :size] += by_query[:split]
                value_acc[:, :size] += by_grad
            height_acc[pl.ds(hbase, hrows), :size] = by_query[split:]

        if head == 0:
            query_grad[...] = jnp.zeros_like(query_grad)
        step(0, True)
        if tiles > 1:

            @pl.loop(1, tiles)
            def _(i):
                step(i, False)

        def merge(full, value):
            if head == 0:
                full[:, low:high] = value
            else:
                full[:, low:high] = jnp.where(mine, value, full[:, low:high])

        merge(key_full, main_acc[:keys, :size] * scale)
        merge(value_full, value_acc[:, :size])
        merge(width_full, main_acc[keys:, :size])
        merge(height_full, height_acc[:, :size])

    width = queries.shape[1]
    sums[...] = jnp.concatenate(
        [key_full[...].reshape(kr, kc, width), value_full[...].reshape(kr, kc, width)], 1
    ).astype(BF16)

    def folded(full):
        value = full[:, 0:HD]
        for head in range(1, HEADS):
            value = value + full[:, head * HD : (head + 1) * HD]
        return value

    tables[...] = jnp.zeros_like(tables)
    r = lax.axis_index("ha")
    w = lax.axis_index("wa")
    fold[...] = folded(height_full)
    per_h = rows_h // STRIDE
    for kh in range(kr):
        at = r + (kr - 1 - kh)
        tables[at // per_h, pl.ds(pl.multiple_of((at % per_h) * STRIDE, STRIDE), STRIDE)] = fold[
            pl.ds(kh, STRIDE, stride=kr)
        ].astype(BF16)
    by_width = folded(width_full)
    per_w = (tables.shape[1] - rows_h) // STRIDE
    for v in range(blocks):
        at = w * pc + (blocks - 1 - v)
        tables[
            at // per_w, pl.ds(pl.multiple_of(rows_h + (at % per_w) * STRIDE, STRIDE), STRIDE)
        ] = by_width[v * STRIDE : (v + 1) * STRIDE].astype(BF16)


def attention(n_ha, n_wa, rows_h, rows_w, queries, out_grad, gathered, height_rows, width_rows):
    own_rows, own_cols, width = queries.shape
    pc = own_cols // STRIDE
    kc = pc * n_wa
    keys = n_ha * kc
    blocks = pc + kc - 1
    tile_rows = max(1, min(own_rows, 256 // own_cols))
    tokens = own_rows * own_cols
    wide = max(window(head)[1] - window(head)[0] for head in range(HEADS))
    vmem = pl.BlockSpec(memory_space=pltpu.VMEM)
    return pl.pallas_call(
        functools.partial(attention_kernel, n_ha, n_wa, pc, own_cols, tile_rows, rows_h),
        out_shape=(
            jax.ShapeDtypeStruct((tokens, width), BF16),
            jax.ShapeDtypeStruct((n_ha, 2 * kc, width), BF16),
            jax.ShapeDtypeStruct((n_ha, rows_h + rows_w, HD), BF16),
        ),
        in_specs=[vmem] * 5,
        out_specs=(vmem,) * 3,
        scratch_shapes=[
            pltpu.VMEM((keys, wide), BF16),
            pltpu.VMEM((keys, wide), BF16),
            pltpu.VMEM((own_rows * n_ha, wide), BF16),
            pltpu.VMEM((blocks * STRIDE, wide), BF16),
            pltpu.VMEM((keys + blocks * STRIDE, wide), F32),
            pltpu.VMEM((own_rows * n_ha, wide), F32),
            pltpu.VMEM((keys, wide), F32),
            pltpu.VMEM((keys, width), F32),
            pltpu.VMEM((keys, width), F32),
            pltpu.VMEM((own_rows * n_ha, width), F32),
            pltpu.VMEM((blocks * STRIDE, width), F32),
            pltpu.VMEM((own_rows * n_ha, HD), F32),
        ],
        compiler_params=pltpu.CompilerParams(vmem_limit_bytes=56 * 2**20),
        name="attention_backward",
    )(queries.reshape(tokens, width), out_grad.reshape(tokens, width), gathered, height_rows, width_rows)


def reduce_kernel(
    n_ha, n_wa, pc,
    sums, tables, cotangent, tables_all,
    sums_in, tables_in, partial, partial_in, slice_out, slice_in,
    sums_send, sums_recv, tables_send, tables_recv,
    own_send, own_recv, below_send, below_recv, slice_send, slice_recv, all_send, all_recv,
):
    r = lax.axis_index("ha")
    w = lax.axis_index("wa")
    kc = pc * n_wa
    has_next = r + 1 < n_ha
    has_prev = r > 0
    barrier = pltpu.get_barrier_semaphore()

    @pl.loop(1, n_ha)
    def _(d):
        pl.semaphore_signal(
            barrier, 1, device_id=(lax.rem(r + d, n_ha), w), device_id_type=MESH
        )

    for d in range(1, n_wa):
        other = lax.rem(w + d, n_wa)
        pl.semaphore_signal(barrier, 1, device_id=(r, other), device_id_type=MESH)

        @pl.when(has_next)
        def _():
            pl.semaphore_signal(barrier, 1, device_id=(r + 1, other), device_id_type=MESH)

        @pl.when(has_prev)
        def _():
            pl.semaphore_signal(barrier, 1, device_id=(r - 1, other), device_id_type=MESH)

    extra = jnp.where(has_next, n_wa - 1, 0) + jnp.where(has_prev, n_wa - 1, 0)
    pl.semaphore_wait(barrier, n_ha - 1 + n_wa - 1 + extra)

    def remote(source, target, send, recv, device):
        return pltpu.make_async_remote_copy(
            src_ref=source, dst_ref=target, send_sem=send, recv_sem=recv,
            device_id=device, device_id_type=MESH,
        )

    def sums_copy(target, slot):
        return remote(
            sums.at[target], sums_in.at[slot], sums_send.at[target], sums_recv.at[slot], (target, w)
        )

    def tables_copy(target, slot):
        return remote(
            tables.at[target], tables_in.at[slot], tables_send.at[target], tables_recv.at[slot],
            (target, w),
        )

    @pl.loop(1, n_ha)
    def _(d):
        target = lax.rem(r + d, n_ha)
        sums_copy(target, r).start()
        tables_copy(target, r).start()

    sums_in[pl.ds(r, 1)] = sums[pl.ds(r, 1)]
    tables_in[pl.ds(r, 1)] = tables[pl.ds(r, 1)]

    @pl.loop(1, n_ha)
    def _(d):
        source = lax.rem(r + n_ha - d, n_ha)
        sums_copy(source, source).wait_recv()
        tables_copy(source, source).wait_recv()

    partial[...] = jnp.sum(sums_in[...].astype(F32), axis=0)
    slice_out[...] = jnp.sum(tables_in[...].astype(F32), axis=0)

    def own_copy(target, slot):
        return remote(
            partial, partial_in.at[0, slot], own_send.at[target], own_recv.at[slot], (r, target)
        )

    def below_copy(target, slot):
        return remote(
            partial, partial_in.at[1, slot], below_send.at[target], below_recv.at[slot],
            (r - 1, target),
        )

    def slice_copy(target, slot):
        return remote(
            slice_out, slice_in.at[slot], slice_send.at[target], slice_recv.at[slot], (r, target)
        )

    for d in range(1, n_wa):
        target = lax.rem(w + d, n_wa)
        slice_copy(target, w).start()
        own_copy(target, w).start()

    @pl.when(has_prev)
    def _():
        for d in range(n_wa):
            below_copy(lax.rem(w + d, n_wa), w).start()

    slice_in[pl.ds(w, 1)] = slice_out[...][None]
    partial_in[0, pl.ds(w, 1)] = partial[...][None]

    for d in range(1, n_wa):
        slice_copy(lax.rem(w + d, n_wa), lax.rem(w + n_wa - d, n_wa)).wait_recv()
    tables_all[pl.ds(r, 1)] = jnp.sum(slice_in[...], axis=0)[None].astype(BF16)

    def all_copy(target, slot):
        return remote(
            tables_all.at[slot], tables_all.at[slot], all_send.at[target], all_recv.at[slot],
            (target, w),
        )

    @pl.loop(1, n_ha)
    def _(d):
        all_copy(lax.rem(r + d, n_ha), r).start()

    @pl.when(jnp.logical_not(has_next))
    def _():
        partial_in[1] = jnp.zeros_like(partial_in[1])

    for d in range(1, n_wa):
        own_copy(lax.rem(w + d, n_wa), lax.rem(w + n_wa - d, n_wa)).wait_recv()

    @pl.when(has_next)
    def _():
        for d in range(n_wa):
            below_copy(lax.rem(w + d, n_wa), lax.rem(w + n_wa - d, n_wa)).wait_recv()

    width = cotangent.shape[-1]
    span = cotangent.shape[2]
    for side in range(2):
        whole = jnp.sum(partial_in[side], axis=0)
        for a in range(2):
            rows = whole[a * kc : (a + 1) * kc]
            chosen = None
            for c in range(n_wa):
                piece = rows[c * pc : min(kc, (c + 1) * pc + 1)]
                piece = jnp.concatenate(
                    [piece, jnp.zeros((span - piece.shape[0], width), F32)], 0
                )
                chosen = piece if chosen is None else jnp.where(w == c, piece, chosen)
            cotangent[side, a] = chosen

    @pl.loop(1, n_ha)
    def _(d):
        target = lax.rem(r + d, n_ha)
        sums_copy(target, r).wait_send()
        tables_copy(target, r).wait_send()

    for d in range(1, n_wa):
        target = lax.rem(w + d, n_wa)
        slice_copy(target, w).wait_send()
        own_copy(target, w).wait_send()

    @pl.when(has_prev)
    def _():
        for d in range(n_wa):
            below_copy(lax.rem(w + d, n_wa), w).wait_send()

    @pl.loop(1, n_ha)
    def _(d):
        source = lax.rem(r + n_ha - d, n_ha)
        all_copy(source, source).wait_recv()

    @pl.loop(1, n_ha)
    def _(d):
        all_copy(lax.rem(r + d, n_ha), r).wait_send()


def reduce_sums(n_ha, n_wa, pc, sums, tables):
    span = round_up(pc + 1, 8)
    rows, width = sums.shape[1:]
    entries = tables.shape[1]
    dma = pltpu.SemaphoreType.DMA
    vmem = pl.BlockSpec(memory_space=pltpu.VMEM)
    return pl.pallas_call(
        functools.partial(reduce_kernel, n_ha, n_wa, pc),
        out_shape=(
            jax.ShapeDtypeStruct((2, 2, span, width), F32),
            jax.ShapeDtypeStruct(tables.shape, BF16),
        ),
        in_specs=[vmem] * 2,
        out_specs=(vmem,) * 2,
        scratch_shapes=[
            pltpu.VMEM((n_ha, rows, width), BF16),
            pltpu.VMEM((n_ha, entries, HD), BF16),
            pltpu.VMEM((rows, width), F32),
            pltpu.VMEM((2, n_wa, rows, width), F32),
            pltpu.VMEM((entries, HD), F32),
            pltpu.VMEM((n_wa, entries, HD), F32),
        ]
        + [dma((n_ha,))] * 4
        + [dma((n_wa,))] * 6
        + [dma((n_ha,))] * 2,
        compiler_params=pltpu.CompilerParams(
            collective_id=1, has_side_effects=True, vmem_limit_bytes=32 * 2**20
        ),
        name="reduce_sums",
    )(sums, tables)


def write_kernel(
    pc, rows_h, cotangent, tables, key_kernel, value_kernel, key_grad, value_grad, height, wide
):
    width = key_grad.shape[-1]
    at = lax.broadcasted_iota(jnp.int32, (STRIDE, 1), 0)
    for a, (kernel, out) in enumerate(((key_kernel, key_grad), (value_kernel, value_grad))):
        out[...] = jnp.zeros_like(out)
        for row, tap, side in ((0, 1, 0), (1, 2, 0), (STRIDE - 1, 0, 1)):
            taps = kernel[tap].astype(F32)
            for k in range(pc):
                here = cotangent[side, a, k : k + 1]
                after = cotangent[side, a, k + 1 : k + 2]
                block = jnp.where(
                    at == 0,
                    here * taps[1:2],
                    jnp.where(
                        at == 1,
                        here * taps[2:3],
                        jnp.where(at == STRIDE - 1, after * taps[0:1], jnp.zeros((STRIDE, width), F32)),
                    ),
                )
                out[row, STRIDE * k : STRIDE * (k + 1)] = block.astype(BF16)
    n_ha = tables.shape[0]
    rows_w = tables.shape[1] - rows_h
    for out, first, size in ((height, 0, rows_h), (wide, rows_h, rows_w)):
        total = out.shape[0]
        for h in range(n_ha):
            count = min(size, total - h * size)
            if count > 0:
                value = tables[h, first : first + size].astype(F32)
                out[h * size : h * size + count] = value[:count]


def write_back(rows_h, cotangent, tables, key_kernel, value_kernel, shape, heights, widths):
    vmem = pl.BlockSpec(memory_space=pltpu.VMEM)
    return pl.pallas_call(
        functools.partial(write_kernel, shape[1] // STRIDE, rows_h),
        out_shape=(
            jax.ShapeDtypeStruct(shape, BF16),
            jax.ShapeDtypeStruct(shape, BF16),
            jax.ShapeDtypeStruct((heights, HD), F32),
            jax.ShapeDtypeStruct((widths, HD), F32),
        ),
        in_specs=[vmem] * 4,
        out_specs=(vmem,) * 4,
        compiler_params=pltpu.CompilerParams(vmem_limit_bytes=32 * 2**20),
        name="write_back",
    )(cotangent, tables, key_kernel, value_kernel)


def on_device(
    queries, key_tokens, value_tokens, out_grad, key_kernel, value_kernel, height_table, width_table
):
    own_rows, own_cols, width = queries.shape
    n_ha = lax.axis_size("ha")
    n_wa = lax.axis_size("wa")
    assert own_rows == STRIDE and own_cols % STRIDE == 0
    pc = own_cols // STRIDE
    kc = pc * n_wa
    blocks = pc + kc - 1
    heights = height_table.shape[0]
    widths = width_table.shape[0]
    rows_h = round_up(-(-heights // n_ha), STRIDE)
    rows_w = round_up(-(-widths // n_ha), STRIDE)
    r = lax.axis_index("ha")
    w = lax.axis_index("wa")
    height_rows = lax.dynamic_slice_in_dim(height_table, r * own_rows, own_rows * n_ha, 0)
    height_rows = height_rows.reshape(n_ha, own_rows, HD)[::-1].transpose(1, 0, 2)
    height_rows = jnp.tile(height_rows.reshape(own_rows * n_ha, HD), (1, HEADS))
    width_rows = lax.dynamic_slice_in_dim(width_table, w * own_cols, blocks * STRIDE, 0)
    width_rows = width_rows.reshape(blocks, STRIDE, HD)[::-1].reshape(blocks * STRIDE, HD)
    width_rows = jnp.tile(width_rows, (1, HEADS))
    gathered = gather_pooled(n_ha, n_wa, key_tokens, value_tokens, key_kernel, value_kernel)
    query_grad, sums, tables = attention(
        n_ha, n_wa, rows_h, rows_w, queries, out_grad, gathered, height_rows, width_rows
    )
    cotangent, tables_all = reduce_sums(n_ha, n_wa, pc, sums, tables)
    key_grad, value_grad, height_grad, width_grad = write_back(
        rows_h, cotangent, tables_all, key_kernel, value_kernel, queries.shape, heights, widths
    )
    return (query_grad.reshape(queries.shape), key_grad, value_grad, height_grad, width_grad)


def solution(mesh):
    placed = (
        P("ha", "wa", None),
        P("ha", "wa", None),
        P("ha", "wa", None),
        P("ha", "wa", None),
        P(),
        P(),
        P(),
        P(),
    )
    return jax.shard_map(
        on_device,
        mesh=mesh,
        in_specs=placed,
        out_specs=(P("ha", "wa", None), P("ha", "wa", None), P("ha", "wa", None), P(), P()),
        check_vma=False,
    )
```

time: 301 us -> 61.9 us (0.21); the launches traced: 297 us -> 61.7 us
  waiting for transfers between devices: 125 us -> 0 us
  blocking collectives: 68.6 us -> 0 us
  Pallas kernels: 0 us -> 53.1 us
  local copies, waits for them, and re-layouts: 42.4 us -> 7.8 us
  matrix products: 34.2 us -> 0 us
  between operations: 14.5 us -> 0.78 us
  starting transfers between devices: 9.44 us -> 0 us
    unnamed x2 -> x0, waiting for transfers between devices: 124 us -> none
    all_gather x1 -> x0, blocking collectives: 68.6 us -> none  [on_device(): gathered = lax.all_gather(flattened, ('ha', 'wa'), axis=1, tiled=True)]
    pallas_call x0 -> x4, Pallas kernels: none -> 53.1 us  [the longest x1 23.5 us: reduce_sums(): pl.pallas_call(functools.partial(reduce_kernel, n_ha, n_wa, pc), out_shap...]
    dot_general x20 -> x0, matrix products: 27.4 us -> none  [the longest x1 4.4 us: on_device(): jnp.einsum('rwnk,rkd->rwnd', grad_height, height_rows.astype(jnp.float32)...]
    dynamic_update_slice x8 -> x0, local copies, waits for them, and re-layouts: 11.2 us -> none  [on_device(): lax.scan(block_step, initial, jnp.arange(block_count, dtype=jnp.int32))]
    reshape x9 -> x0, local copies, waits for them, and re-layouts: 10.7 us -> none  [the longest x1 3.27 us: on_device(): query_flat = queries.reshape(token_count, HEADS, HD)]
    ppermute x4 -> x0, starting transfers between devices: 9.41 us -> none  [from_behind(): return lax.ppermute(block, axis, route)]
    conv_general_dilated x4 -> x0, matrix products: 3.84 us -> none  [pool_partial(): lax.conv_general_dilated(tokens[None], kernel.astype(jnp.float32)[:, :, N...]
  transfers between devices with their start and end apart: 5 -> 0, of which waited for: 2 -> 0; matrix products, arithmetic and copies ran while one was open for 10% -> 0% of each run, Pallas kernels for 0% -> 0%
where the time goes in v1:
time: 61.9 us; the launch traced here: 61.7 us
  Pallas kernels  53.1 us (86%)
  local copies, waits for them, and re-layouts  7.8 us (13%)
  between operations  0.78 us (1%)
    pallas_call x1, Pallas kernels, reduce_sums(): pl.pallas_call(functools.partial(reduce_kernel, n_ha, n_wa, pc), out_shap...  23.5 us
    pallas_call x1, Pallas kernels, gather_pooled(): pl.pallas_call(functools.partial(gather_kernel, n_ha, n_wa, pc), out_shap...  14.4 us
    pallas_call x1, Pallas kernels, attention(): pl.pallas_call(functools.partial(attention_kernel, n_ha, n_wa, pc, own_co...  13.9 us
    unnamed x22, local copies, waits for them, and re-layouts  5.81 us
    pallas_call x1, Pallas kernels, write_back(): pl.pallas_call(functools.partial(write_kernel, shape[1] // STRIDE, rows_h...  1.31 us

profile of v1, /device:TPU:0, one launch (start us, length us, event | category | flops | bytes accessed | tf_op | source)
XLA Modules:
  0.0 61.7 jit_solution(13743536577298134323)
XLA Ops:
  0.6 0.0 copy-start
  0.7 0.9 %copy-done = bf16[511,96]{0,1:T(8,128)(2,1)S(1)} copy-done((bf16[511,96]{0,1:T(8,128)(2,1)S(1)}, bf16[511,96]{0,1:T(8,128)(2,1)}, u32[]{:S(2)}) %copy-start) | copy-done | bytes 98136
  1.5 0.1 constant_dynamic-slice_fusion.1
  1.6 0.1 copy.27
  1.8 0.0 copy-start.8
  1.8 0.0 copy-start.7
  1.8 0.0 copy-start.1
  1.8 0.0 copy-start.2
  1.8 0.1 copy.22
  1.9 0.6 %copy-done.8 = bf16[255,96]{0,1:T(8,128)(2,1)S(1)} copy-done((bf16[255,96]{0,1:T(8,128)(2,1)S(1)}, bf16[255,96]{0,1:T(8,128)(2,1)}, u32[]{:S(2)}) %copy-start.8) | copy-done | bytes 48984
  2.6 0.1 constant_dynamic-slice_fusion
  2.6 0.1 copy.28
  2.8 0.1 tile.24
  2.8 0.8 %tile.25.width_rows = bf16[176,384]{1,0:T(8,128)(2,1)} reshape(bf16[176,4,96]{2,1,0:T(4,128)(2,1)S(1)} %tile.24) | data formatting | bytes 270336 | tf_op jit(solution)/shard_map/tile | solution.py:707
  3.7 0.0 copy-start.6
  3.7 0.8 %copy.24.height_rows = bf16[256,384]{1,0:T(8,128)(2,1)} copy(bf16[256,384]{0,1:T(8,128)(2,1)S(1)} %bitcast.10) | data formatting | bytes 393216 | tf_op jit(solution)/shard_map/tile | solution.py:704
  4.5 0.0 copy-done.7
  4.5 0.0 copy-done.1
  4.5 0.0 copy-done.2
  4.5 0.0 copy-done.6
  4.5 14.4 %pool_gather.1.gathered = bf16[16,16,384]{2,1,0:T(8,128)(2,1)S(1)} custom-call(bf16[16,64,384]{2,1,0:T(8,128)(2,1)S(1)} %copy-done.1, bf16[16,64,384]{2,1,0:T(8,128)(2,1)S(1)} %copy-done.2, bf16[3,3,384]{2,1,0:T(4,128)(2,1)S(1)} %copy-done.6, bf16[3,3,384]{2,1,0:T(4,128)(2,1)S(1)} %copy-done.7), custom_call_target="tpu_custom_call" | custom-call | tf_op jit(solution)/shard_map/pool_gather/pallas_call | solution.py:197
  18.9 0.0 copy-start.3
  18.9 0.7 %copy-done.3 = bf16[16,16,384]{2,1,0:T(8,128)(2,1)} copy-done((bf16[16,16,384]{2,1,0:T(8,128)(2,1)}, bf16[16,16,384]{2,1,0:T(8,128)(2,1)S(1)}, u32[]{:S(2)}) %copy-start.3) | copy-done | bytes 196632
  19.6 13.9 %attention_backward.1 = (bf16[1024,384]{1,0:T(8,128)(2,1)}, bf16[16,16,384]{2,1,0:T(8,128)(2,1)}, bf16[16,48,96]{2,1,0:T(8,128)(2,1)}) custom-call(bf16[1024,384]{1,0:T(8,128)(2,1)} %bitcast.11, bf16[1024,384]{1,0:T(8,128)(2,1)} %bitcast.12, bf16[16,16,384]{2,1,0:T(8,128)(2,1)} %copy-done.3, bf16[256,384]{1,0:T(8,128)(2,1)} %copy.24.height_rows, ...), custom_call_target="tpu_custom_call" | custom-call | tf_op jit(solution)/shard_map/attention_backward/pallas_call | solution.py:410
  33.5 0.0 copy-start.4
  33.5 0.9 %copy-done.4 = bf16[16,16,384]{2,1,0:T(8,128)(2,1)S(1)} copy-done((bf16[16,16,384]{2,1,0:T(8,128)(2,1)S(1)}, bf16[16,16,384]{2,1,0:T(8,128)(2,1)}, u32[]{:S(2)}) %copy-start.4) | copy-done | bytes 196632
  34.4 0.0 copy-start.5
  34.4 0.9 %copy-done.5 = bf16[16,48,96]{2,1,0:T(8,128)(2,1)S(1)} copy-done((bf16[16,48,96]{2,1,0:T(8,128)(2,1)S(1)}, bf16[16,48,96]{2,1,0:T(8,128)(2,1)}, u32[]{:S(2)}) %copy-start.5) | copy-done | bytes 147480
  35.4 23.5 %reduce_sums.1 = (f32[2,2,8,384]{3,2,1,0:T(8,128)S(1)}, bf16[16,48,96]{2,1,0:T(8,128)(2,1)S(1)}) custom-call(bf16[16,16,384]{2,1,0:T(8,128)(2,1)S(1)} %copy-done.4, bf16[16,48,96]{2,1,0:T(8,128)(2,1)S(1)} %copy-done.5), custom_call_target="tpu_custom_call" | custom-call | tf_op jit(solution)/shard_map/reduce_sums/pallas_call | solution.py:610
  58.8 1.3 %write_back.1 = (bf16[16,64,384]{2,1,0:T(8,128)(2,1)}, bf16[16,64,384]{2,1,0:T(8,128)(2,1)}, f32[511,96]{1,0:T(8,128)S(1)}, f32[255,96]{1,0:T(8,128)S(1)}) custom-call(f32[2,2,8,384]{3,2,1,0:T(8,128)S(1)} %get-tuple-element.17.cotangent, bf16[16,48,96]{2,1,0:T(8,128)(2,1)S(1)} %get-tuple-element.18.tables, bf16[3,3,384]{2,1,0:T(4,128)(2,1)S(1)} %copy-done.6, ...), custom_call_target="tpu_custom_call" | custom-call | tf_op jit(solution)/shard_map/write_back/pallas_call | solution.py:671
  60.2 0.7 %copy.26 = f32[255,96]{0,1:T(8,128)} copy(f32[255,96]{1,0:T(8,128)S(1)} %get-tuple-element.37) | data formatting | bytes 195840
  60.9 0.8 %copy.25 = f32[511,96]{0,1:T(8,128)} copy(f32[511,96]{1,0:T(8,128)S(1)} %get-tuple-element.36) | data formatting | bytes 392448
  (4 shorter events, 0.0 us)
Async XLA Ops:
  0.6 0.9 %copy-start = (bf16[511,96]{0,1:T(8,128)(2,1)S(1)}, bf16[511,96]{0,1:T(8,128)(2,1)}, u32[]{:S(2)}) copy-start(bf16[511,96]{0,1:T(8,128)(2,1)} %param.14) | copy-start | bytes 294340
  1.8 0.8 %copy-start.8 = (bf16[255,96]{0,1:T(8,128)(2,1)S(1)}, bf16[255,96]{0,1:T(8,128)(2,1)}, u32[]{:S(2)}) copy-start(bf16[255,96]{0,1:T(8,128)(2,1)} %param.15) | copy-start | bytes 146884
  1.8 2.7 %copy-start.7 = (bf16[3,3,384]{2,1,0:T(4,128)(2,1)S(1)}, bf16[3,3,384]{2,1,0:T(4,128)(2,1)}, u32[]{:S(2)}) copy-start(bf16[3,3,384]{2,1,0:T(4,128)(2,1)} %value_kernel.3) | copy-start | bytes 20740
  1.8 2.7 %copy-start.1 = (bf16[16,64,384]{2,1,0:T(8,128)(2,1)S(1)}, bf16[16,64,384]{2,1,0:T(8,128)(2,1)}, u32[]{:S(2)}) copy-start(bf16[16,64,384]{2,1,0:T(8,128)(2,1)} %key_hbm.1) | copy-start | bytes 2359300
  1.8 2.7 %copy-start.2 = (bf16[16,64,384]{2,1,0:T(8,128)(2,1)S(1)}, bf16[16,64,384]{2,1,0:T(8,128)(2,1)}, u32[]{:S(2)}) copy-start(bf16[16,64,384]{2,1,0:T(8,128)(2,1)} %value_hbm.1) | copy-start | bytes 2359300
  3.7 0.8 %copy-start.6 = (bf16[3,3,384]{2,1,0:T(4,128)(2,1)S(1)}, bf16[3,3,384]{2,1,0:T(4,128)(2,1)}, u32[]{:S(2)}) copy-start(bf16[3,3,384]{2,1,0:T(4,128)(2,1)} %key_kernel.3) | copy-start | bytes 20740
  18.9 0.7 %copy-start.3 = (bf16[16,16,384]{2,1,0:T(8,128)(2,1)}, bf16[16,16,384]{2,1,0:T(8,128)(2,1)S(1)}, u32[]{:S(2)}) copy-start(bf16[16,16,384]{2,1,0:T(8,128)(2,1)S(1)} %pool_gather.1.gathered) | copy-start | bytes 589828
  33.5 0.9 %copy-start.4 = (bf16[16,16,384]{2,1,0:T(8,128)(2,1)S(1)}, bf16[16,16,384]{2,1,0:T(8,128)(2,1)}, u32[]{:S(2)}) copy-start(bf16[16,16,384]{2,1,0:T(8,128)(2,1)} %get-tuple-element.15.sums) | copy-start | bytes 589828
  34.4 0.9 %copy-start.5 = (bf16[16,48,96]{2,1,0:T(8,128)(2,1)S(1)}, bf16[16,48,96]{2,1,0:T(8,128)(2,1)}, u32[]{:S(2)}) copy-start(bf16[16,48,96]{2,1,0:T(8,128)(2,1)} %get-tuple-element.16.tables) | copy-start | bytes 442372

commit v2 on v1

--- a/solution.py
+++ b/solution.py
@@ -20,16 +20,10 @@
     return -(-value // unit) * unit
 
 
-def greet(to_each, count):
-    barrier = pltpu.get_barrier_semaphore()
-    to_each(lambda device: pl.semaphore_signal(barrier, 1, device_id=device, device_id_type=MESH))
-    pl.semaphore_wait(barrier, count)
-
-
-def gather_kernel(
+def gather_part(
     n_ha, n_wa, pc,
     key_hbm, value_hbm, key_kernel, value_kernel, gathered,
-    tokens, part, arrived, load_sem, own_send, own_recv, next_send, next_recv, row_send, row_recv,
+    tokens, part, arrived, load_sem, own_send, own_recv, next_send, next_recv, row_send, row_recv, prepare,
 ):
     r = lax.axis_index("ha")
     w = lax.axis_index("wa")
@@ -131,6 +125,7 @@
             next_copy(lax.rem(w + d, n_wa), w).start()
 
     arrived[0, pl.ds(w, 1)] = part[0:1]
+    prepare()
 
     @pl.when(r == 0)
     def _():
@@ -189,36 +184,6 @@
         row_copy(lax.rem(r + d, n_ha), r).wait_send()
 
 
-def gather_pooled(n_ha, n_wa, key_tokens, value_tokens, key_kernel, value_kernel):
-    own_cols, width = key_tokens.shape[1:]
-    pc = own_cols // STRIDE
-    span = round_up(pc + 1, 8)
-    dma = pltpu.SemaphoreType.DMA
-    return pl.pallas_call(
-        functools.partial(gather_kernel, n_ha, n_wa, pc),
-        out_shape=jax.ShapeDtypeStruct((n_ha, 2 * pc * n_wa, width), BF16),
-        in_specs=[pl.BlockSpec(memory_space=pl.ANY)] * 2
-        + [pl.BlockSpec(memory_space=pltpu.VMEM)] * 2,
-        out_specs=pl.BlockSpec(memory_space=pltpu.VMEM),
-        scratch_shapes=[
-            pltpu.VMEM((2, 3, own_cols, width), BF16),
-            pltpu.VMEM((2, 2, span, width), F32),
-            pltpu.VMEM((2, n_wa, 2, span, width), F32),
-            dma((4,)),
-            dma((n_wa,)),
-            dma((n_wa,)),
-            dma((n_wa,)),
-            dma((n_wa,)),
-            dma((n_ha,)),
-            dma((n_ha,)),
-        ],
-        compiler_params=pltpu.CompilerParams(
-            collective_id=0, has_side_effects=True, vmem_limit_bytes=32 * 2**20
-        ),
-        name="pool_gather",
-    )(key_tokens, value_tokens, key_kernel, value_kernel)
-
-
 def window(head):
     low = head * HD // 128 * 128
     high = round_up((head + 1) * HD, 128)
@@ -237,10 +202,10 @@
     return lax.dot_general(left, right, (((0,), (0,)), ((), ())), preferred_element_type=F32)
 
 
-def attention_kernel(
+def attention_part(
     n_ha, n_wa, pc, own_cols, tile_rows, rows_h,
     queries, out_grad, gathered, height_rows, width_rows,
-    query_grad, sums, tables,
+    query_grad, sums, tables_h, tables_w, send_lanes,
     key_win, value_win, height_win, width_win, main_acc, height_acc, value_acc,
     key_full, value_full, height_full, width_full, fold,
 ):
@@ -366,11 +331,17 @@
         merge(value_full, value_acc[:, :size])
         merge(width_full, main_acc[keys:, :size])
         merge(height_full, height_acc[:, :size])
-
-    width = queries.shape[1]
-    sums[...] = jnp.concatenate(
-        [key_full[...].reshape(kr, kc, width), value_full[...].reshape(kr, kc, width)], 1
-    ).astype(BF16)
+        for t in range(queries.shape[1] // 128):
+            if head == -(-128 * (t + 1) // HD) - 1:
+                lanes = slice(128 * t, 128 * (t + 1))
+                sums[t] = jnp.concatenate(
+                    [
+                        key_full[:, lanes].reshape(kr, kc, 128),
+                        value_full[:, lanes].reshape(kr, kc, 128),
+                    ],
+                    1,
+                ).astype(BF16)
+                send_lanes(t)
 
     def folded(full):
         value = full[:, 0:HD]
@@ -378,68 +349,38 @@
             value = value + full[:, head * HD : (head + 1) * HD]
         return value
 
-    tables[...] = jnp.zeros_like(tables)
+    tables_h[...] = jnp.zeros_like(tables_h)
+    tables_w[...] = jnp.zeros_like(tables_w)
     r = lax.axis_index("ha")
     w = lax.axis_index("wa")
     fold[...] = folded(height_full)
     per_h = rows_h // STRIDE
     for kh in range(kr):
         at = r + (kr - 1 - kh)
-        tables[at // per_h, pl.ds(pl.multiple_of((at % per_h) * STRIDE, STRIDE), STRIDE)] = fold[
+        tables_h[at // per_h, pl.ds(pl.multiple_of((at % per_h) * STRIDE, STRIDE), STRIDE)] = fold[
             pl.ds(kh, STRIDE, stride=kr)
         ].astype(BF16)
     by_width = folded(width_full)
-    per_w = (tables.shape[1] - rows_h) // STRIDE
+    per_w = tables_w.shape[1] // STRIDE
     for v in range(blocks):
         at = w * pc + (blocks - 1 - v)
-        tables[
-            at // per_w, pl.ds(pl.multiple_of(rows_h + (at % per_w) * STRIDE, STRIDE), STRIDE)
-        ] = by_width[v * STRIDE : (v + 1) * STRIDE].astype(BF16)
-
-
-def attention(n_ha, n_wa, rows_h, rows_w, queries, out_grad, gathered, height_rows, width_rows):
-    own_rows, own_cols, width = queries.shape
-    pc = own_cols // STRIDE
-    kc = pc * n_wa
-    keys = n_ha * kc
-    blocks = pc + kc - 1
-    tile_rows = max(1, min(own_rows, 256 // own_cols))
-    tokens = own_rows * own_cols
-    wide = max(window(head)[1] - window(head)[0] for head in range(HEADS))
-    vmem = pl.BlockSpec(memory_space=pltpu.VMEM)
-    return pl.pallas_call(
-        functools.partial(attention_kernel, n_ha, n_wa, pc, own_cols, tile_rows, rows_h),
-        out_shape=(
-            jax.ShapeDtypeStruct((tokens, width), BF16),
-            jax.ShapeDtypeStruct((n_ha, 2 * kc, width), BF16),
-            jax.ShapeDtypeStruct((n_ha, rows_h + rows_w, HD), BF16),
-        ),
-        in_specs=[vmem] * 5,
-        out_specs=(vmem,) * 3,
-        scratch_shapes=[
-            pltpu.VMEM((keys, wide), BF16),
-            pltpu.VMEM((keys, wide), BF16),
-            pltpu.VMEM((own_rows * n_ha, wide), BF16),
-            pltpu.VMEM((blocks * STRIDE, wide), BF16),
-            pltpu.VMEM((keys + blocks * STRIDE, wide), F32),
-            pltpu.VMEM((own_rows * n_ha, wide), F32),
-            pltpu.VMEM((keys, wide), F32),
-            pltpu.VMEM((keys, width), F32),
-            pltpu.VMEM((keys, width), F32),
-            pltpu.VMEM((own_rows * n_ha, width), F32),
-            pltpu.VMEM((blocks * STRIDE, width), F32),
-            pltpu.VMEM((own_rows * n_ha, HD), F32),
-        ],
-        compiler_params=pltpu.CompilerParams(vmem_limit_bytes=56 * 2**20),
-        name="attention_backward",
-    )(queries.reshape(tokens, width), out_grad.reshape(tokens, width), gathered, height_rows, width_rows)
-
-
-def reduce_kernel(
-    n_ha, n_wa, pc,
-    sums, tables, cotangent, tables_all,
-    sums_in, tables_in, partial, partial_in, slice_out, slice_in,
-    sums_send, sums_recv, tables_send, tables_recv,
+        tables_w[at // per_w, pl.ds(pl.multiple_of((at % per_w) * STRIDE, STRIDE), STRIDE)] = (
+            by_width[v * STRIDE : (v + 1) * STRIDE].astype(BF16)
+        )
+
+
+def remote(source, target, send, recv, device):
+    return pltpu.make_async_remote_copy(
+        src_ref=source, dst_ref=target, send_sem=send, recv_sem=recv,
+        device_id=device, device_id_type=MESH,
+    )
+
+
+def reduce_part(
+    n_ha, n_wa, pc, sums_copy,
+    sums, tables_h, tables_w, cotangent, tables_all,
+    sums_in, tables_h_in, tables_w_in, partial, partial_in, slice_out, slice_in,
+    h_send, h_recv, w_send, w_recv,
     own_send, own_recv, below_send, below_recv, slice_send, slice_recv, all_send, all_recv,
 ):
     r = lax.axis_index("ha")
@@ -447,63 +388,56 @@
     kc = pc * n_wa
     has_next = r + 1 < n_ha
     has_prev = r > 0
-    barrier = pltpu.get_barrier_semaphore()
-
-    @pl.loop(1, n_ha)
-    def _(d):
-        pl.semaphore_signal(
-            barrier, 1, device_id=(lax.rem(r + d, n_ha), w), device_id_type=MESH
-        )
-
-    for d in range(1, n_wa):
-        other = lax.rem(w + d, n_wa)
-        pl.semaphore_signal(barrier, 1, device_id=(r, other), device_id_type=MESH)
-
-        @pl.when(has_next)
+    lanes = sums.shape[0]
+    rows_h = tables_h.shape[1]
+    rows_w = tables_w.shape[1]
+    per_h = rows_h // STRIDE
+    per_w = rows_w // STRIDE
+    blocks = pc + kc - 1
+
+    def meets_h(source, owner):
+        return (per_h * owner + per_h > source) & (per_h * owner < source + n_ha)
+
+    def meets_w(owner):
+        return (per_w * owner + per_w > pc * w) & (per_w * owner < pc * w + blocks)
+
+    def h_copy(target, slot):
+        return remote(
+            tables_h.at[target], tables_h_in.at[slot], h_send.at[target], h_recv.at[slot],
+            (target, w),
+        )
+
+    def w_copy(target, slot):
+        return remote(
+            tables_w.at[target], tables_w_in.at[slot], w_send.at[target], w_recv.at[slot],
+            (target, w),
+        )
+
+    @pl.loop(1, n_ha)
+    def _(d):
+        target = lax.rem(r + d, n_ha)
+
+        @pl.when(meets_h(r, target))
         def _():
-            pl.semaphore_signal(barrier, 1, device_id=(r + 1, other), device_id_type=MESH)
-
-        @pl.when(has_prev)
+            h_copy(target, r).start()
+
+        @pl.when(meets_w(target))
         def _():
-            pl.semaphore_signal(barrier, 1, device_id=(r - 1, other), device_id_type=MESH)
-
-    extra = jnp.where(has_next, n_wa - 1, 0) + jnp.where(has_prev, n_wa - 1, 0)
-    pl.semaphore_wait(barrier, n_ha - 1 + n_wa - 1 + extra)
-
-    def remote(source, target, send, recv, device):
-        return pltpu.make_async_remote_copy(
-            src_ref=source, dst_ref=target, send_sem=send, recv_sem=recv,
-            device_id=device, device_id_type=MESH,
-        )
-
-    def sums_copy(target, slot):
-        return remote(
-            sums.at[target], sums_in.at[slot], sums_send.at[target], sums_recv.at[slot], (target, w)
-        )
-
-    def tables_copy(target, slot):
-        return remote(
-            tables.at[target], tables_in.at[slot], tables_send.at[target], tables_recv.at[slot],
-            (target, w),
-        )
-
-    @pl.loop(1, n_ha)
-    def _(d):
-        target = lax.rem(r + d, n_ha)
-        sums_copy(target, r).start()
-        tables_copy(target, r).start()
-
-    sums_in[pl.ds(r, 1)] = sums[pl.ds(r, 1)]
-    tables_in[pl.ds(r, 1)] = tables[pl.ds(r, 1)]
+            w_copy(target, r).start()
+
+    for t in range(lanes):
+        sums_in[t, pl.ds(r, 1)] = sums[t, pl.ds(r, 1)]
+    tables_h_in[pl.ds(r, 1)] = tables_h[pl.ds(r, 1)]
+    tables_w_in[pl.ds(r, 1)] = tables_w[pl.ds(r, 1)]
 
     @pl.loop(1, n_ha)
     def _(d):
         source = lax.rem(r + n_ha - d, n_ha)
-        sums_copy(source, source).wait_recv()
-        tables_copy(source, source).wait_recv()
-
-    partial[...] = jnp.sum(sums_in[...].astype(F32), axis=0)
-    slice_out[...] = jnp.sum(tables_in[...].astype(F32), axis=0)
+        for t in range(lanes):
+            sums_copy(t, source, source).wait_recv()
+
+    for t in range(lanes):
+        partial[:, 128 * t : 128 * (t + 1)] = jnp.sum(sums_in[t].astype(F32), axis=0)
 
     def own_copy(target, slot):
         return remote(
@@ -522,14 +456,30 @@
         )
 
     for d in range(1, n_wa):
-        target = lax.rem(w + d, n_wa)
-        slice_copy(target, w).start()
-        own_copy(target, w).start()
+        own_copy(lax.rem(w + d, n_wa), w).start()
 
     @pl.when(has_prev)
     def _():
         for d in range(n_wa):
             below_copy(lax.rem(w + d, n_wa), w).start()
+
+    @pl.loop(1, n_ha)
+    def _(d):
+        source = lax.rem(r + n_ha - d, n_ha)
+
+        @pl.when(meets_h(source, r))
+        def _():
+            h_copy(source, source).wait_recv()
+
+        @pl.when(meets_w(r))
+        def _():
+            w_copy(source, source).wait_recv()
+
+    slice_out[0:rows_h] = jnp.sum(tables_h_in[...].astype(F32), axis=0)
+    slice_out[rows_h:] = jnp.sum(tables_w_in[...].astype(F32), axis=0)
+
+    for d in range(1, n_wa):
+        slice_copy(lax.rem(w + d, n_wa), w).start()
 
     slice_in[pl.ds(w, 1)] = slice_out[...][None]
     partial_in[0, pl.ds(w, 1)] = partial[...][None]
@@ -578,8 +528,16 @@
     @pl.loop(1, n_ha)
     def _(d):
         target = lax.rem(r + d, n_ha)
-        sums_copy(target, r).wait_send()
-        tables_copy(target, r).wait_send()
+        for t in range(lanes):
+            sums_copy(t, target, r).wait_send()
+
+        @pl.when(meets_h(r, target))
+        def _():
+            h_copy(target, r).wait_send()
+
+        @pl.when(meets_w(target))
+        def _():
+            w_copy(target, r).wait_send()
 
     for d in range(1, n_wa):
         target = lax.rem(w + d, n_wa)
@@ -601,46 +559,176 @@
         all_copy(lax.rem(r + d, n_ha), r).wait_send()
 
 
-def reduce_sums(n_ha, n_wa, pc, sums, tables):
+def fused_kernel(
+    n_ha, n_wa, pc, own_cols, tile_rows, rows_h,
+    key_hbm, value_hbm, query_hbm, grad_hbm, key_kernel, value_kernel, height_table, width_table,
+    query_out, cotangent, tables_all,
+    queries, out_grad, query_grad, gathered, sums, tables_h, tables_w, sums_in, tables_h_in,
+    tables_w_in, height_float, height_rows, width_rows, big_send, sums_send, sums_recv,
+    *rest,
+):
+    gather_refs, attention_refs, reduce_refs = rest[:10], rest[10:22], rest[22:]
+    r = lax.axis_index("ha")
+    w = lax.axis_index("wa")
+    kc = pc * n_wa
+    blocks = pc + kc - 1
+    fetch = [
+        pltpu.make_async_copy(query_hbm, queries, big_send.at[0]),
+        pltpu.make_async_copy(grad_hbm, out_grad, big_send.at[1]),
+    ]
+    tables_h_in[...] = jnp.zeros_like(tables_h_in)
+    tables_w_in[...] = jnp.zeros_like(tables_w_in)
+
+    def prepare():
+        for copy in fetch:
+            copy.start()
+        for v in range(n_ha):
+            start = pl.multiple_of(r * STRIDE + v * STRIDE, STRIDE)
+            height_float[pl.ds(n_ha - 1 - v, STRIDE, stride=n_ha)] = height_table[
+                pl.ds(start, STRIDE)
+            ].astype(F32)
+        once = height_float[...]
+        height_rows[...] = jnp.concatenate([once] * HEADS, 1).astype(BF16)
+        for v in range(blocks):
+            start = pl.multiple_of(w * own_cols + v * STRIDE, STRIDE)
+            once = width_table[pl.ds(start, STRIDE)].astype(F32)
+            width_rows[(blocks - 1 - v) * STRIDE : (blocks - v) * STRIDE] = jnp.concatenate(
+                [once] * HEADS, 1
+            ).astype(BF16)
+
+    gather_part(
+        n_ha, n_wa, pc, key_hbm, value_hbm, key_kernel, value_kernel, gathered, *gather_refs,
+        prepare,
+    )
+    for copy in fetch:
+        copy.wait()
+
+    def sums_copy(t, target, slot):
+        return remote(
+            sums.at[t, target], sums_in.at[t, slot], sums_send.at[t, target], sums_recv.at[t, slot],
+            (target, w),
+        )
+
+    def send_lanes(t):
+        @pl.loop(1, n_ha)
+        def _(d):
+            sums_copy(t, lax.rem(r + d, n_ha), r).start()
+
+    attention_part(
+        n_ha, n_wa, pc, own_cols, tile_rows, rows_h,
+        queries, out_grad, gathered, height_rows, width_rows,
+        query_grad, sums, tables_h, tables_w, send_lanes, *attention_refs,
+    )
+    put = pltpu.make_async_copy(query_grad, query_out, big_send.at[2])
+    put.start()
+    reduce_part(
+        n_ha, n_wa, pc, sums_copy, sums, tables_h, tables_w, cotangent, tables_all,
+        sums_in, tables_h_in, tables_w_in, *reduce_refs,
+    )
+    put.wait()
+
+
+def fused(
+    n_ha, n_wa, rows_h, rows_w,
+    queries, key_tokens, value_tokens, out_grad, key_kernel, value_kernel, height_table, width_table,
+):
+    own_rows, own_cols, width = queries.shape
+    pc = own_cols // STRIDE
+    kc = pc * n_wa
+    keys = n_ha * kc
+    blocks = pc + kc - 1
     span = round_up(pc + 1, 8)
-    rows, width = sums.shape[1:]
-    entries = tables.shape[1]
+    lanes = width // 128
+    entries = rows_h + rows_w
+    tile_rows = max(1, min(own_rows, 256 // own_cols))
+    tokens = own_rows * own_cols
+    wide = max(window(head)[1] - window(head)[0] for head in range(HEADS))
+    vmem = pl.BlockSpec(memory_space=pltpu.VMEM)
+    anywhere = pl.BlockSpec(memory_space=pl.ANY)
     dma = pltpu.SemaphoreType.DMA
-    vmem = pl.BlockSpec(memory_space=pltpu.VMEM)
+    ram = pltpu.VMEM
     return pl.pallas_call(
-        functools.partial(reduce_kernel, n_ha, n_wa, pc),
+        functools.partial(fused_kernel, n_ha, n_wa, pc, own_cols, tile_rows, rows_h),
         out_shape=(
+            jax.ShapeDtypeStruct((tokens, width), BF16),
             jax.ShapeDtypeStruct((2, 2, span, width), F32),
-            jax.ShapeDtypeStruct(tables.shape, BF16),
+            jax.ShapeDtypeStruct((n_ha, entries, HD), BF16),
         ),
-        in_specs=[vmem] * 2,
-        out_specs=(vmem,) * 2,
+        in_specs=[anywhere] * 4 + [vmem] * 4,
+        out_specs=(anywhere, vmem, vmem),
         scratch_shapes=[
-            pltpu.VMEM((n_ha, rows, width), BF16),
-            pltpu.VMEM((n_ha, entries, HD), BF16),
-            pltpu.VMEM((rows, width), F32),
-            pltpu.VMEM((2, n_wa, rows, width), F32),
-            pltpu.VMEM((entries, HD), F32),
-            pltpu.VMEM((n_wa, entries, HD), F32),
+            ram((tokens, width), BF16),
+            ram((tokens, width), BF16),
+            ram((tokens, width), BF16),
+            ram((n_ha, 2 * kc, width), BF16),
+            ram((lanes, n_ha, 2 * kc, 128), BF16),
+            ram((n_ha, rows_h, HD), BF16),
+            ram((n_ha, rows_w, HD), BF16),
+            ram((lanes, n_ha, 2 * kc, 128), BF16),
+            ram((n_ha, rows_h, HD), BF16),
+            ram((n_ha, rows_w, HD), BF16),
+            ram((own_rows * n_ha, HD), F32),
+            ram((own_rows * n_ha, width), BF16),
+            ram((blocks * STRIDE, width), BF16),
+            dma((3,)),
+            dma((lanes, n_ha)),
+            dma((lanes, n_ha)),
+            ram((2, 3, own_cols, width), BF16),
+            ram((2, 2, span, width), F32),
+            ram((2, n_wa, 2, span, width), F32),
+            dma((4,)),
+            dma((n_wa,)),
+            dma((n_wa,)),
+            dma((n_wa,)),
+            dma((n_wa,)),
+            dma((n_ha,)),
+            dma((n_ha,)),
+            ram((keys, wide), BF16),
+            ram((keys, wide), BF16),
+            ram((own_rows * n_ha, wide), BF16),
+            ram((blocks * STRIDE, wide), BF16),
+            ram((keys + blocks * STRIDE, wide), F32),
+            ram((own_rows * n_ha, wide), F32),
+            ram((keys, wide), F32),
+            ram((keys, width), F32),
+            ram((keys, width), F32),
+            ram((own_rows * n_ha, width), F32),
+            ram((blocks * STRIDE, width), F32),
+            ram((own_rows * n_ha, HD), F32),
+            ram((2 * kc, width), F32),
+            ram((2, n_wa, 2 * kc, width), F32),
+            ram((entries, HD), F32),
+            ram((n_wa, entries, HD), F32),
         ]
         + [dma((n_ha,))] * 4
         + [dma((n_wa,))] * 6
         + [dma((n_ha,))] * 2,
         compiler_params=pltpu.CompilerParams(
-            collective_id=1, has_side_effects=True, vmem_limit_bytes=32 * 2**20
+            collective_id=0, has_side_effects=True, vmem_limit_bytes=56 * 2**20
         ),
-        name="reduce_sums",
-    )(sums, tables)
+        name="pooled_attention",
+    )(
+        key_tokens, value_tokens, queries.reshape(tokens, width), out_grad.reshape(tokens, width),
+        key_kernel, value_kernel, height_table, width_table,
+    )
 
 
 def write_kernel(
-    pc, rows_h, cotangent, tables, key_kernel, value_kernel, key_grad, value_grad, height, wide
+    pc, rows_h, cotangent, tables, key_kernel, value_kernel, key_out, value_out, height, wide,
+    middle, edges, done,
 ):
-    width = key_grad.shape[-1]
+    width = edges.shape[-1]
+    middle[...] = jnp.zeros_like(middle)
+    copies = []
+    for a, out in enumerate((key_out, value_out)):
+        copies.append(
+            pltpu.make_async_copy(middle, out.at[pl.ds(2, STRIDE - 3)], done.at[3 * a])
+        )
+        copies[-1].start()
+    edges[...] = jnp.zeros_like(edges)
     at = lax.broadcasted_iota(jnp.int32, (STRIDE, 1), 0)
-    for a, (kernel, out) in enumerate(((key_kernel, key_grad), (value_kernel, value_grad))):
-        out[...] = jnp.zeros_like(out)
-        for row, tap, side in ((0, 1, 0), (1, 2, 0), (STRIDE - 1, 0, 1)):
+    for a, (kernel, out) in enumerate(((key_kernel, key_out), (value_kernel, value_out))):
+        for row, tap, side in ((0, 1, 0), (1, 2, 0), (2, 0, 1)):
             taps = kernel[tap].astype(F32)
             for k in range(pc):
                 here = cotangent[side, a, k : k + 1]
@@ -654,7 +742,17 @@
                         jnp.where(at == STRIDE - 1, after * taps[0:1], jnp.zeros((STRIDE, width), F32)),
                     ),
                 )
-                out[row, STRIDE * k : STRIDE * (k + 1)] = block.astype(BF16)
+                edges[a, row, STRIDE * k : STRIDE * (k + 1)] = block.astype(BF16)
+        copies.append(
+            pltpu.make_async_copy(edges.at[a, pl.ds(0, 2)], out.at[pl.ds(0, 2)], done.at[3 * a + 1])
+        )
+        copies[-1].start()
+        copies.append(
+            pltpu.make_async_copy(
+                edges.at[a, pl.ds(2, 1)], out.at[pl.ds(STRIDE - 1, 1)], done.at[3 * a + 2]
+            )
+        )
+        copies[-1].start()
     n_ha = tables.shape[0]
     rows_w = tables.shape[1] - rows_h
     for out, first, size in ((height, 0, rows_h), (wide, rows_h, rows_w)):
@@ -664,6 +762,8 @@
             if count > 0:
                 value = tables[h, first : first + size].astype(F32)
                 out[h * size : h * size + count] = value[:count]
+    for copy in copies:
+        copy.wait()
 
 
 def write_back(rows_h, cotangent, tables, key_kernel, value_kernel, shape, heights, widths):
@@ -677,7 +777,12 @@
             jax.ShapeDtypeStruct((widths, HD), F32),
         ),
         in_specs=[vmem] * 4,
-        out_specs=(vmem,) * 4,
+        out_specs=(pl.BlockSpec(memory_space=pl.ANY),) * 2 + (vmem,) * 2,
+        scratch_shapes=[
+            pltpu.VMEM((STRIDE - 3,) + shape[1:], BF16),
+            pltpu.VMEM((2, 3) + shape[1:], BF16),
+            pltpu.SemaphoreType.DMA((6,)),
+        ],
         compiler_params=pltpu.CompilerParams(vmem_limit_bytes=32 * 2**20),
         name="write_back",
     )(cotangent, tables, key_kernel, value_kernel)
@@ -690,26 +795,15 @@
     n_ha = lax.axis_size("ha")
     n_wa = lax.axis_size("wa")
     assert own_rows == STRIDE and own_cols % STRIDE == 0
-    pc = own_cols // STRIDE
-    kc = pc * n_wa
-    blocks = pc + kc - 1
     heights = height_table.shape[0]
     widths = width_table.shape[0]
     rows_h = round_up(-(-heights // n_ha), STRIDE)
     rows_w = round_up(-(-widths // n_ha), STRIDE)
-    r = lax.axis_index("ha")
-    w = lax.axis_index("wa")
-    height_rows = lax.dynamic_slice_in_dim(height_table, r * own_rows, own_rows * n_ha, 0)
-    height_rows = height_rows.reshape(n_ha, own_rows, HD)[::-1].transpose(1, 0, 2)
-    height_rows = jnp.tile(height_rows.reshape(own_rows * n_ha, HD), (1, HEADS))
-    width_rows = lax.dynamic_slice_in_dim(width_table, w * own_cols, blocks * STRIDE, 0)
-    width_rows = width_rows.reshape(blocks, STRIDE, HD)[::-1].reshape(blocks * STRIDE, HD)
-    width_rows = jnp.tile(width_rows, (1, HEADS))
-    gathered = gather_pooled(n_ha, n_wa, key_tokens, value_tokens, key_kernel, value_kernel)
-    query_grad, sums, tables = attention(
-        n_ha, n_wa, rows_h, rows_w, queries, out_grad, gathered, height_rows, width_rows
+    query_grad, cotangent, tables_all = fused(
+        n_ha, n_wa, rows_h, rows_w,
+        queries, key_tokens, value_tokens, out_grad, key_kernel, value_kernel, height_table,
+        width_table,
     )
-    cotangent, tables_all = reduce_sums(n_ha, n_wa, pc, sums, tables)
     key_grad, value_grad, height_grad, width_grad = write_back(
         rows_h, cotangent, tables_all, key_kernel, value_kernel, queries.shape, heights, widths
     )

time: 61.9 us -> 52.6 us (0.85)
  Pallas kernels: 53.1 us -> 45.2 us
  local copies, waits for them, and re-layouts: 7.8 us -> 6.47 us
    pallas_call x3 -> x1, Pallas kernels: 51.8 us -> 43.9 us  [fused(): pl.pallas_call(functools.partial(fused_kernel, n_ha, n_wa, pc, own_cols,...]
    another operation x5 -> x0, local copies, waits for them, and re-layouts: 1.79 us -> none  [the longest x3 0.93 us: on_device(): height_rows = jnp.tile(height_rows.reshape(own_rows * n_ha, HD), (1, HEADS))]
    unnamed x22 -> x17, local copies, waits for them, and re-layouts: 5.81 us -> 6.47 us
where the time goes in v2:
time: 52.6 us; the launch traced here: 52.3 us
  Pallas kernels  45.2 us (86%)
  local copies, waits for them, and re-layouts  6.47 us (12%)
  between operations  0.69 us (1%)
    pallas_call x1, Pallas kernels, fused(): pl.pallas_call(functools.partial(fused_kernel, n_ha, n_wa, pc, own_cols,...  43.9 us
    unnamed x17, local copies, waits for them, and re-layouts  6.47 us
    pallas_call x1, Pallas kernels, write_back(): pl.pallas_call(functools.partial(write_kernel, shape[1] // STRIDE, rows_h...  1.23 us

profile of v2, /device:TPU:0, one launch (start us, length us, event | category | flops | bytes accessed | tf_op | source)
XLA Modules:
  0.0 52.3 jit_solution(7577325669190613606)
XLA Ops:
  0.6 0.0 copy-start.5
  0.6 1.6 %copy.14.width_table = bf16[255,96]{1,0:T(8,128)(2,1)} copy(bf16[255,96]{0,1:T(8,128)(2,1)} %param.15) | data formatting | bytes 97920 | tf_op args[7]
  2.2 0.0 copy-done.5
  2.2 0.8 %copy.13.height_table = bf16[511,96]{1,0:T(8,128)(2,1)} copy(bf16[511,96]{0,1:T(8,128)(2,1)S(1)} %copy-done.5) | data formatting | bytes 196224 | tf_op args[6]
  3.0 0.0 copy-start.2
  3.0 0.0 copy-start.3
  3.0 43.9 %pooled_attention.1 = (bf16[1024,384]{1,0:T(8,128)(2,1)}, f32[2,2,8,384]{3,2,1,0:T(8,128)}, bf16[16,48,96]{2,1,0:T(8,128)(2,1)}) custom-call(bf16[16,64,384]{2,1,0:T(8,128)(2,1)} %key_hbm.1, bf16[16,64,384]{2,1,0:T(8,128)(2,1)} %value_hbm.1, bf16[1024,384]{1,0:T(8,128)(2,1)} %bitcast.4, bf16[1024,384]{1,0:T(8,128)(2,1)} %bitcast.5, ...), custom_call_target="tpu_custom_call" | custom-call | tf_op jit(solution)/shard_map/pooled_attention/pallas_call | solution.py:650
  46.9 0.0 copy-done.2
  46.9 0.0 copy-done.3
  46.9 0.0 copy-start
  47.0 0.9 %copy-done = bf16[16,48,96]{2,1,0:T(8,128)(2,1)S(1)} copy-done((bf16[16,48,96]{2,1,0:T(8,128)(2,1)S(1)}, bf16[16,48,96]{2,1,0:T(8,128)(2,1)}, u32[]{:S(2)}) %copy-start) | copy-done | bytes 147480
  47.9 0.0 copy-start.1
  47.9 0.8 %copy-done.1 = f32[2,2,8,384]{3,2,1,0:T(8,128)S(1)} copy-done((f32[2,2,8,384]{3,2,1,0:T(8,128)S(1)}, f32[2,2,8,384]{3,2,1,0:T(8,128)}, u32[]{:S(2)}) %copy-start.1) | copy-done | bytes 49176
  48.7 0.0 copy-start.4
  48.7 1.2 %write_back.1 = (bf16[16,64,384]{2,1,0:T(8,128)(2,1)}, bf16[16,64,384]{2,1,0:T(8,128)(2,1)}, f32[511,96]{1,0:T(8,128)S(1)}, f32[255,96]{1,0:T(8,128)S(1)}) custom-call(f32[2,2,8,384]{3,2,1,0:T(8,128)S(1)} %copy-done.1, bf16[16,48,96]{2,1,0:T(8,128)(2,1)S(1)} %copy-done, bf16[3,3,384]{2,1,0:T(4,128)(2,1)S(1)} %copy-done.2, bf16[3,3,384]{2,1,0:T(4,128)(2,1)S(1)} %copy-done.3), custom_call_target="tpu_custom_call" | custom-call | tf_op jit(solution)/shard_map/write_back/pallas_call | solution.py:771
  49.9 0.7 %copy.16 = f32[255,96]{0,1:T(8,128)} copy(f32[255,96]{1,0:T(8,128)S(1)} %get-tuple-element.23) | data formatting | bytes 195840
  50.6 0.8 %copy.15 = f32[511,96]{0,1:T(8,128)} copy(f32[511,96]{1,0:T(8,128)S(1)} %get-tuple-element.22) | data formatting | bytes 392448
  51.4 0.0 copy-done.4
  51.4 0.9 %copy.18 = bf16[16,64,384]{2,1,0:T(8,128)(2,1)} copy(bf16[16,64,384]{2,1,0:T(8,128)(2,1)S(1)} %bitcast.3) | data formatting | bytes 1572864
Async XLA Ops:
  0.6 1.6 %copy-start.5 = (bf16[511,96]{0,1:T(8,128)(2,1)S(1)}, bf16[511,96]{0,1:T(8,128)(2,1)}, u32[]{:S(2)}) copy-start(bf16[511,96]{0,1:T(8,128)(2,1)} %param.14) | copy-start | bytes 294340
  3.0 44.0 %copy-start.2 = (bf16[3,3,384]{2,1,0:T(4,128)(2,1)S(1)}, bf16[3,3,384]{2,1,0:T(4,128)(2,1)}, u32[]{:S(2)}) copy-start(bf16[3,3,384]{2,1,0:T(4,128)(2,1)} %key_kernel.3) | copy-start | bytes 20740
  3.0 44.0 %copy-start.3 = (bf16[3,3,384]{2,1,0:T(4,128)(2,1)S(1)}, bf16[3,3,384]{2,1,0:T(4,128)(2,1)}, u32[]{:S(2)}) copy-start(bf16[3,3,384]{2,1,0:T(4,128)(2,1)} %value_kernel.3) | copy-start | bytes 20740
  46.9 0.9 %copy-start = (bf16[16,48,96]{2,1,0:T(8,128)(2,1)S(1)}, bf16[16,48,96]{2,1,0:T(8,128)(2,1)}, u32[]{:S(2)}) copy-start(bf16[16,48,96]{2,1,0:T(8,128)(2,1)} %get-tuple-element.14.tables) | copy-start | bytes 442372
  47.9 0.8 %copy-start.1 = (f32[2,2,8,384]{3,2,1,0:T(8,128)S(1)}, f32[2,2,8,384]{3,2,1,0:T(8,128)}, u32[]{:S(2)}) copy-start(f32[2,2,8,384]{3,2,1,0:T(8,128)} %get-tuple-element.13.cotangent) | copy-start | bytes 147460
  48.7 2.8 %copy-start.4 = (bf16[1024,384]{1,0:T(8,128)(2,1)S(1)}, bf16[1024,384]{1,0:T(8,128)(2,1)}, u32[]{:S(2)}) copy-start(bf16[1024,384]{1,0:T(8,128)(2,1)} %get-tuple-element.12) | copy-start | bytes 2359300

commit v3 on v2

--- a/solution.py
+++ b/solution.py
@@ -250,8 +250,9 @@
             vw_ = value_win[:, :size]
             hw_ = height_win[pl.ds(hbase, hrows), :size]
             ww_ = width_win[:, :size]
-            raw_h = nt(hw_, q)
-            raw_w = nt(ww_, q)
+            raw = nt(jnp.concatenate([kw_, ww_, hw_], 0), q)
+            raw_w = raw[keys : keys + blocks * STRIDE]
+            raw_h = raw[keys + blocks * STRIDE :]
             rel_h = raw_h[0:kr]
             for a in range(1, tile_rows):
                 rel_h = jnp.where(lane_row == a, raw_h[a * kr : (a + 1) * kr], rel_h)
@@ -261,7 +262,7 @@
             rel_w = picked[pc - 1 : pc - 1 + kc]
             for u in range(1, pc):
                 rel_w = jnp.where(lane_block == u, picked[pc - 1 - u : pc - 1 - u + kc], rel_w)
-            scores = nt(kw_, q).reshape(kr, kc, tile) * scale + (rel_h[:, None, :] + rel_w[None])
+            scores = raw[:keys].reshape(kr, kc, tile) * scale + (rel_h[:, None, :] + rel_w[None])
             top = jnp.max(jnp.max(scores, axis=0), axis=0, keepdims=True)
             weights = jnp.exp(scores - top[None])
             total = jnp.sum(jnp.sum(weights, axis=0), axis=0, keepdims=True)
@@ -317,7 +318,7 @@
         step(0, True)
         if tiles > 1:
 
-            @pl.loop(1, tiles)
+            @pl.loop(1, tiles, unroll=tiles - 1 if keys <= 256 else 1)
             def _(i):
                 step(i, False)
 
@@ -564,7 +565,7 @@
     key_hbm, value_hbm, query_hbm, grad_hbm, key_kernel, value_kernel, height_table, width_table,
     query_out, cotangent, tables_all,
     queries, out_grad, query_grad, gathered, sums, tables_h, tables_w, sums_in, tables_h_in,
-    tables_w_in, height_float, height_rows, width_rows, big_send, sums_send, sums_recv,
+    tables_w_in, flat_h, flat_w, turned_h, turned_w, height_float, height_rows, width_rows, big_send, sums_send, sums_recv,
     *rest,
 ):
     gather_refs, attention_refs, reduce_refs = rest[:10], rest[10:22], rest[22:]
@@ -582,16 +583,23 @@
     def prepare():
         for copy in fetch:
             copy.start()
+        for table, flat, turned in (
+            (height_table, flat_h, turned_h),
+            (width_table, flat_w, turned_w),
+        ):
+            flat[...] = jnp.zeros_like(flat)
+            flat[:, : table.shape[1]] = table[...].astype(F32)
+            turned[...] = flat[...].T
         for v in range(n_ha):
             start = pl.multiple_of(r * STRIDE + v * STRIDE, STRIDE)
-            height_float[pl.ds(n_ha - 1 - v, STRIDE, stride=n_ha)] = height_table[
+            height_float[pl.ds(n_ha - 1 - v, STRIDE, stride=n_ha)] = turned_h[
                 pl.ds(start, STRIDE)
-            ].astype(F32)
+            ]
         once = height_float[...]
         height_rows[...] = jnp.concatenate([once] * HEADS, 1).astype(BF16)
         for v in range(blocks):
             start = pl.multiple_of(w * own_cols + v * STRIDE, STRIDE)
-            once = width_table[pl.ds(start, STRIDE)].astype(F32)
+            once = turned_w[pl.ds(start, STRIDE)]
             width_rows[(blocks - 1 - v) * STRIDE : (blocks - v) * STRIDE] = jnp.concatenate(
                 [once] * HEADS, 1
             ).astype(BF16)
@@ -667,6 +675,10 @@
             ram((lanes, n_ha, 2 * kc, 128), BF16),
             ram((n_ha, rows_h, HD), BF16),
             ram((n_ha, rows_w, HD), BF16),
+            ram((HD, round_up(height_table.shape[1], 128)), F32),
+            ram((HD, round_up(width_table.shape[1], 128)), F32),
+            ram((round_up(height_table.shape[1], 128), HD), F32),
+            ram((round_up(width_table.shape[1], 128), HD), F32),
             ram((own_rows * n_ha, HD), F32),
             ram((own_rows * n_ha, width), BF16),
             ram((blocks * STRIDE, width), BF16),
@@ -714,18 +726,26 @@
 
 
 def write_kernel(
-    pc, rows_h, cotangent, tables, key_kernel, value_kernel, key_out, value_out, height, wide,
-    middle, edges, done,
+    pc, rows_h, cotangent_hbm, tables_hbm, query_in, key_kernel, value_kernel,
+    query_out, key_out, value_out, height, wide,
+    middle, edges, cotangent, tables, loaded, done,
 ):
     width = edges.shape[-1]
+    loads = [
+        pltpu.make_async_copy(cotangent_hbm, cotangent, loaded.at[0]),
+        pltpu.make_async_copy(tables_hbm, tables, loaded.at[1]),
+    ]
+    copies = [pltpu.make_async_copy(query_in, query_out, done.at[6])]
+    for copy in loads + copies:
+        copy.start()
     middle[...] = jnp.zeros_like(middle)
-    copies = []
     for a, out in enumerate((key_out, value_out)):
         copies.append(
             pltpu.make_async_copy(middle, out.at[pl.ds(2, STRIDE - 3)], done.at[3 * a])
         )
         copies[-1].start()
     edges[...] = jnp.zeros_like(edges)
+    loads[0].wait()
     at = lax.broadcasted_iota(jnp.int32, (STRIDE, 1), 0)
     for a, (kernel, out) in enumerate(((key_kernel, key_out), (value_kernel, value_out))):
         for row, tap, side in ((0, 1, 0), (1, 2, 0), (2, 0, 1)):
@@ -753,39 +773,42 @@
             )
         )
         copies[-1].start()
+    loads[1].wait()
     n_ha = tables.shape[0]
-    rows_w = tables.shape[1] - rows_h
-    for out, first, size in ((height, 0, rows_h), (wide, rows_h, rows_w)):
-        total = out.shape[0]
-        for h in range(n_ha):
-            count = min(size, total - h * size)
-            if count > 0:
-                value = tables[h, first : first + size].astype(F32)
-                out[h * size : h * size + count] = value[:count]
+    for out, first, last in ((height, 0, rows_h), (wide, rows_h, tables.shape[1])):
+        value = tables[:, first:last].astype(F32).reshape(n_ha * (last - first), HD)
+        out[...] = value.T[:, : out.shape[1]]
     for copy in copies:
         copy.wait()
 
 
-def write_back(rows_h, cotangent, tables, key_kernel, value_kernel, shape, heights, widths):
+def write_back(
+    rows_h, cotangent, tables, query_grad, key_kernel, value_kernel, shape, heights, widths
+):
     vmem = pl.BlockSpec(memory_space=pltpu.VMEM)
+    anywhere = pl.BlockSpec(memory_space=pl.ANY)
     return pl.pallas_call(
         functools.partial(write_kernel, shape[1] // STRIDE, rows_h),
         out_shape=(
+            jax.ShapeDtypeStruct(query_grad.shape, BF16),
             jax.ShapeDtypeStruct(shape, BF16),
             jax.ShapeDtypeStruct(shape, BF16),
-            jax.ShapeDtypeStruct((heights, HD), F32),
-            jax.ShapeDtypeStruct((widths, HD), F32),
+            jax.ShapeDtypeStruct((HD, heights), F32),
+            jax.ShapeDtypeStruct((HD, widths), F32),
         ),
-        in_specs=[vmem] * 4,
-        out_specs=(pl.BlockSpec(memory_space=pl.ANY),) * 2 + (vmem,) * 2,
+        in_specs=[anywhere] * 3 + [vmem] * 2,
+        out_specs=(anywhere,) * 3 + (vmem,) * 2,
         scratch_shapes=[
             pltpu.VMEM((STRIDE - 3,) + shape[1:], BF16),
             pltpu.VMEM((2, 3) + shape[1:], BF16),
-            pltpu.SemaphoreType.DMA((6,)),
+            pltpu.VMEM(cotangent.shape, F32),
+            pltpu.VMEM(tables.shape, BF16),
+            pltpu.SemaphoreType.DMA((2,)),
+            pltpu.SemaphoreType.DMA((7,)),
         ],
-        compiler_params=pltpu.CompilerParams(vmem_limit_bytes=32 * 2**20),
+        compiler_params=pltpu.CompilerParams(vmem_limit_bytes=56 * 2**20),
         name="write_back",
-    )(cotangent, tables, key_kernel, value_kernel)
+    )(cotangent, tables, query_grad, key_kernel, value_kernel)
 
 
 def on_device(
@@ -801,13 +824,16 @@
     rows_w = round_up(-(-widths // n_ha), STRIDE)
     query_grad, cotangent, tables_all = fused(
         n_ha, n_wa, rows_h, rows_w,
-        queries, key_tokens, value_tokens, out_grad, key_kernel, value_kernel, height_table,
-        width_table,
-    )
-    key_grad, value_grad, height_grad, width_grad = write_back(
-        rows_h, cotangent, tables_all, key_kernel, value_kernel, queries.shape, heights, widths
-    )
-    return (query_grad.reshape(queries.shape), key_grad, value_grad, height_grad, width_grad)
+        queries, key_tokens, value_tokens, out_grad, key_kernel, value_kernel, height_table.T,
+        width_table.T,
+    )
+    query_grad, key_grad, value_grad, height_grad, width_grad = write_back(
+        rows_h, cotangent, tables_all, query_grad, key_kernel, value_kernel, queries.shape,
+        heights, widths,
+    )
+    return (
+        query_grad.reshape(queries.shape), key_grad, value_grad, height_grad.T, width_grad.T
+    )
 
 
 def solution(mesh):

time: 52.6 us -> 68.7 us (1.31)
  Pallas kernels: 45.2 us -> 67.8 us
  local copies, waits for them, and re-layouts: 6.47 us -> 0 us
    pallas_call x1, Pallas kernels: 1.23 us -> 26.4 us  [write_back(): pl.pallas_call(functools.partial(write_kernel, shape[1] // STRIDE, rows_h...]
    unnamed x17 -> x0, local copies, waits for them, and re-layouts: 6.47 us -> none
    pallas_call x1, Pallas kernels: 43.9 us -> 41.3 us  [fused(): pl.pallas_call(functools.partial(fused_kernel, n_ha, n_wa, pc, own_cols,...]
where the time goes in v3:
time: 68.7 us; the launch traced here: 68.4 us
  Pallas kernels  67.8 us (99%)
    pallas_call x1, Pallas kernels, fused(): pl.pallas_call(functools.partial(fused_kernel, n_ha, n_wa, pc, own_cols,...  41.3 us
    pallas_call x1, Pallas kernels, write_back(): pl.pallas_call(functools.partial(write_kernel, shape[1] // STRIDE, rows_h...  26.4 us

profile of v3, /device:TPU:0, one launch (start us, length us, event | category | flops | bytes accessed | tf_op | source)
XLA Modules:
  0.0 68.4 jit_solution(14346915687167642750)
XLA Ops:
  0.6 41.3 %pooled_attention.1 = (bf16[1024,384]{1,0:T(8,128)(2,1)}, f32[2,2,8,384]{3,2,1,0:T(8,128)}, bf16[16,48,96]{2,1,0:T(8,128)(2,1)}) custom-call(bf16[16,64,384]{2,1,0:T(8,128)(2,1)} %key_hbm.1, bf16[16,64,384]{2,1,0:T(8,128)(2,1)} %value_hbm.1, bf16[1024,384]{1,0:T(8,128)(2,1)} %bitcast.7, bf16[1024,384]{1,0:T(8,128)(2,1)} %bitcast.8, ...), custom_call_target="tpu_custom_call" | custom-call | tf_op jit(solution)/shard_map/pooled_attention/pallas_call | solution.py:658
  42.0 26.4 %write_back.1 = (bf16[1024,384]{1,0:T(8,128)(2,1)}, bf16[16,64,384]{2,1,0:T(8,128)(2,1)}, bf16[16,64,384]{2,1,0:T(8,128)(2,1)}, f32[96,511]{1,0:T(8,128)}, f32[96,255]{1,0:T(8,128)}) custom-call(f32[2,2,8,384]{3,2,1,0:T(8,128)} %get-tuple-element.13.cotangent_hbm, bf16[16,48,96]{2,1,0:T(8,128)(2,1)} %get-tuple-element.14.tables_hbm, ...), custom_call_target="tpu_custom_call" | custom-call | tf_op jit(solution)/shard_map/write_back/pallas_call | solution.py:790

commit v4 on v3

--- a/solution.py
+++ b/solution.py
@@ -728,15 +728,16 @@
 def write_kernel(
     pc, rows_h, cotangent_hbm, tables_hbm, query_in, key_kernel, value_kernel,
     query_out, key_out, value_out, height, wide,
-    middle, edges, cotangent, tables, loaded, done,
+    middle, edges, cotangent, tables, passed, loaded, done,
 ):
     width = edges.shape[-1]
     loads = [
         pltpu.make_async_copy(cotangent_hbm, cotangent, loaded.at[0]),
         pltpu.make_async_copy(tables_hbm, tables, loaded.at[1]),
+        pltpu.make_async_copy(query_in, passed, loaded.at[2]),
     ]
-    copies = [pltpu.make_async_copy(query_in, query_out, done.at[6])]
-    for copy in loads + copies:
+    copies = []
+    for copy in loads:
         copy.start()
     middle[...] = jnp.zeros_like(middle)
     for a, out in enumerate((key_out, value_out)):
@@ -773,6 +774,9 @@
             )
         )
         copies[-1].start()
+    loads[2].wait()
+    copies.append(pltpu.make_async_copy(passed, query_out, done.at[6]))
+    copies[-1].start()
     loads[1].wait()
     n_ha = tables.shape[0]
     for out, first, last in ((height, 0, rows_h), (wide, rows_h, tables.shape[1])):
@@ -803,7 +807,8 @@
             pltpu.VMEM((2, 3) + shape[1:], BF16),
             pltpu.VMEM(cotangent.shape, F32),
             pltpu.VMEM(tables.shape, BF16),
-            pltpu.SemaphoreType.DMA((2,)),
+            pltpu.VMEM(query_grad.shape, BF16),
+            pltpu.SemaphoreType.DMA((3,)),
             pltpu.SemaphoreType.DMA((7,)),
         ],
         compiler_params=pltpu.CompilerParams(vmem_limit_bytes=56 * 2**20),

time: 68.7 us -> 46.4 us (0.68)
  Pallas kernels: 67.8 us -> 45.4 us
    pallas_call x1, Pallas kernels: 26.4 us -> 4.12 us  [write_back(): pl.pallas_call(functools.partial(write_kernel, shape[1] // STRIDE, rows_h...]
where the time goes in v4:
time: 46.4 us; the launch traced here: 46.1 us
  Pallas kernels  45.4 us (98%)
  between operations  0.64 us (1%)
    pallas_call x1, Pallas kernels, fused(): pl.pallas_call(functools.partial(fused_kernel, n_ha, n_wa, pc, own_cols,...  41.3 us
    pallas_call x1, Pallas kernels, write_back(): pl.pallas_call(functools.partial(write_kernel, shape[1] // STRIDE, rows_h...  4.12 us

profile of v4, /device:TPU:0, one launch (start us, length us, event | category | flops | bytes accessed | tf_op | source)
XLA Modules:
  0.0 46.1 jit_solution(1815881548280530443)
XLA Ops:
  0.6 41.3 %pooled_attention.1 = (bf16[1024,384]{1,0:T(8,128)(2,1)}, f32[2,2,8,384]{3,2,1,0:T(8,128)}, bf16[16,48,96]{2,1,0:T(8,128)(2,1)}) custom-call(bf16[16,64,384]{2,1,0:T(8,128)(2,1)} %key_hbm.1, bf16[16,64,384]{2,1,0:T(8,128)(2,1)} %value_hbm.1, bf16[1024,384]{1,0:T(8,128)(2,1)} %bitcast.7, bf16[1024,384]{1,0:T(8,128)(2,1)} %bitcast.8, ...), custom_call_target="tpu_custom_call" | custom-call | tf_op jit(solution)/shard_map/pooled_attention/pallas_call | solution.py:658
  42.0 4.1 %write_back.1 = (bf16[1024,384]{1,0:T(8,128)(2,1)}, bf16[16,64,384]{2,1,0:T(8,128)(2,1)}, bf16[16,64,384]{2,1,0:T(8,128)(2,1)}, f32[96,511]{1,0:T(8,128)}, f32[96,255]{1,0:T(8,128)}) custom-call(f32[2,2,8,384]{3,2,1,0:T(8,128)} %get-tuple-element.13.cotangent_hbm, bf16[16,48,96]{2,1,0:T(8,128)(2,1)} %get-tuple-element.14.tables_hbm, ...), custom_call_target="tpu_custom_call" | custom-call | tf_op jit(solution)/shard_map/write_back/pallas_call | solution.py:794
